TPU v7x, 32 devices: a whole 2x2x4 slice. The times are simulated.
32 devices in a mesh: slab: 4 (over y, core), plane: 8 (over z, x).
Axes of the slice: x: 2, y: 2, z: 4, core: 2. Of those that a mesh axis runs over, the one named last changes fastest.
Arguments:
- start_disp: float32 [3, 64, 128, 128], P(None, 'slab', 'plane'), may hold values from -6 to 6
- load: float32 [3, 64, 128, 128], P(None, 'slab', 'plane'), may hold values from -6 to 6
- shift: float32 [64, 128, 128], P('slab', 'plane'), may hold values from 0.25 to 2
- coarse: float32 [3, 32, 64, 128], P(None, 'slab', 'plane'), may hold values from -6 to 6
- aggregate: int32 [64, 128], P('slab', 'plane'), may hold values from 0 to 2047, as said below
- consistency: float32 [64, 128, 128], P('slab', 'plane'), may hold values from 0.5 to 2
Outputs:
- displacement: float32 [3, 64, 128, 128], P(None, 'slab', 'plane')
- recovered: float32 [6, 64, 128, 128], P(None, 'slab', 'plane')
- indicator: float32 [64, 128, 128], P('slab', 'plane')
Inputs may be any that keep to these rules, and one draw needn't show every extreme that they name: aggregate[i, j] = a * 64 + b with |a - i // 2| <= 1 and |b - j // 2| <= 1.
All inputs are finite; a program needn't handle non-finite values.
Results may differ from a plain program's by a relative error of at most 0.000029.
Values sent between devices are 32-bit elements; how exact they have to be, the bound alone decides.
A program may use at most 64 MiB of HBM per device.

v0:
```python
import jax
import jax.numpy as jnp
from jax import lax
from jax.sharding import PartitionSpec as P

DEGREE = 4


THETA = 4.5
DELTA_C = 3.5


def extended(block, sides, width):
    for axis, dim in sides:
        count = lax.axis_size(axis)
        forward = [(i, i + 1) for i in range(count - 1)]
        backward = [(target, source) for source, target in forward]
        low = lax.ppermute(
            lax.slice_in_dim(block, block.shape[dim] - width, None, axis=dim), axis, forward
        )
        high = lax.ppermute(lax.slice_in_dim(block, 0, width, axis=dim), axis, backward)
        block = jnp.concatenate([low, block, high], axis=dim)
    return block


def stiff_apply(padded, shift_part):
    zpad = jnp.pad(padded, ((0, 0), (0, 0), (0, 0), (1, 1)))
    along_z = zpad[..., :-2] + zpad[..., 1:-1] + zpad[..., 2:]
    along_x = along_z[:, :-2] + along_z[:, 1:-1] + along_z[:, 2:]
    boxed = along_x[:, :, :-2] + along_x[:, :, 1:-1] + along_x[:, :, 2:]
    centre = padded[:, 1:-1, 1:-1]
    return (3.0 + shift_part) * centre - boxed / 3.0


def element_stress(corners, consist):
    zpad = jnp.pad(corners, ((0, 0), (0, 0), (0, 0), (0, 1)))
    diff_x = zpad[:, 1:] - zpad[:, :-1]
    grad_x = 0.25 * (
        diff_x[:, :, :-1, :-1]
        + diff_x[:, :, 1:, :-1]
        + diff_x[:, :, :-1, 1:]
        + diff_x[:, :, 1:, 1:]
    )
    diff_y = zpad[:, :, 1:] - zpad[:, :, :-1]
    grad_y = 0.25 * (
        diff_y[:, :-1, :, :-1]
        + diff_y[:, 1:, :, :-1]
        + diff_y[:, :-1, :, 1:]
        + diff_y[:, 1:, :, 1:]
    )
    diff_z = zpad[..., 1:] - zpad[..., :-1]
    grad_z = 0.25 * (
        diff_z[:, :-1, :-1] + diff_z[:, 1:, :-1] + diff_z[:, :-1, 1:] + diff_z[:, 1:, 1:]
    )
    exx = grad_x[0]
    eyy = grad_y[1]
    ezz = grad_z[2]
    exy = 0.5 * (grad_y[0] + grad_x[1])
    eyz = 0.5 * (grad_z[1] + grad_y[2])
    ezx = 0.5 * (grad_x[2] + grad_z[0])
    trace = exx + eyy + ezz
    sxx = exx - trace / 3.0
    syy = eyy - trace / 3.0
    szz = ezz - trace / 3.0
    equiv = (
        2.0 / 3.0 * (sxx * sxx + syy * syy + szz * szz + 2.0 * (exy * exy + eyz * eyz + ezx * ezx))
    )
    visc = consist * (0.01 + 3.0 * equiv) ** ((0.15 - 1.0) / 2.0)
    sig = [
        2.0 * visc * sxx + 4.0 * trace,
        2.0 * visc * syy + 4.0 * trace,
        2.0 * visc * szz + 4.0 * trace,
        2.0 * visc * exy,
        2.0 * visc * eyz,
        2.0 * visc * ezx,
    ]
    norm_sq = (
        sig[0] * sig[0]
        + sig[1] * sig[1]
        + sig[2] * sig[2]
        + 2.0 * (sig[3] * sig[3] + sig[4] * sig[4] + sig[5] * sig[5])
    )
    return jnp.stack(sig + [norm_sq], 0)


def corner_valid(start_x, start_y, rows_x, rows_y, total_x, total_y, depth):
    gx = start_x + jnp.arange(rows_x)[:, None, None]
    gy = start_y + jnp.arange(rows_y)[None, :, None]
    gz = jnp.arange(depth)[None, None, :]
    return (
        (gx >= 0) & (gx <= total_x - 2) & (gy >= 0) & (gy <= total_y - 2) & (gz <= depth - 2)
    ).astype(jnp.float32)


def prolong_local(start_disp, coarse, aggregate):
    rows_x, rows_y, depth = (start_disp.shape[1], start_disp.shape[2], start_disp.shape[3])
    coarse_x, coarse_y = (coarse.shape[1], coarse.shape[2])
    coarse_cols = coarse_y * lax.axis_size("plane")
    wide_coarse = extended(coarse, (("slab", 1), ("plane", 2)), 1)
    local_a = aggregate // coarse_cols - (lax.axis_index("slab") * coarse_x - 1)
    local_b = aggregate % coarse_cols - (lax.axis_index("plane") * coarse_y - 1)
    flat = (local_a * (coarse_y + 2) + local_b).reshape(-1)
    table = wide_coarse.reshape(3, (coarse_x + 2) * (coarse_y + 2), depth)
    moved = jnp.take(table, flat, axis=1).reshape(3, rows_x, rows_y, depth)
    return start_disp + moved


def body(start_disp, load, shift, coarse, aggregate, consistency):
    rows_x, rows_y, depth = (start_disp.shape[1], start_disp.shape[2], start_disp.shape[3])
    total_x = rows_x * lax.axis_size("slab")
    total_y = rows_y * lax.axis_size("plane")
    first_x = lax.axis_index("slab") * rows_x
    first_y = lax.axis_index("plane") * rows_y
    sigma = THETA / DELTA_C
    disp = prolong_local(start_disp, coarse, aggregate)

    def stiff(field):
        padded = extended(field, (("slab", 1), ("plane", 2)), 1)
        return stiff_apply(padded, shift)

    resid = load - stiff(disp)
    direction = resid / THETA
    rho = 1.0 / sigma
    for step in range(DEGREE):
        disp = disp + direction
        if step < DEGREE - 1:
            resid = resid - stiff(direction)
            rho_new = 1.0 / (2.0 * sigma - rho)
            direction = rho_new * rho * direction + 2.0 * rho_new / DELTA_C * resid
            rho = rho_new
    ghosted = extended(
        jnp.concatenate([disp, consistency[None]], 0), (("slab", 1), ("plane", 2)), 1
    )
    near = ghosted[0:3]
    near_consist = ghosted[3]
    valid = corner_valid(first_x - 1, first_y - 1, rows_x + 1, rows_y + 1, total_x, total_y, depth)
    elem = element_stress(near, near_consist[: rows_x + 1, : rows_y + 1]) * valid
    sum_x = elem[:, 1:] + elem[:, :-1]
    sum_y = sum_x[:, :, 1:] + sum_x[:, :, :-1]
    front = jnp.pad(sum_y, ((0, 0), (0, 0), (0, 0), (1, 0)))
    total = front[..., 1:] + front[..., :-1]
    gx = first_x + jnp.arange(rows_x)[:, None, None]
    gy = first_y + jnp.arange(rows_y)[None, :, None]
    gz = jnp.arange(depth)[None, None, :]
    count = (
        ((gx >= 1).astype(jnp.float32) + (gx <= total_x - 2).astype(jnp.float32))
        * ((gy >= 1).astype(jnp.float32) + (gy <= total_y - 2).astype(jnp.float32))
        * ((gz >= 1).astype(jnp.float32) + (gz <= depth - 2).astype(jnp.float32))
    )
    rec = total[:6] / count
    norm_rec = (
        rec[0] * rec[0]
        + rec[1] * rec[1]
        + rec[2] * rec[2]
        + 2.0 * (rec[3] * rec[3] + rec[4] * rec[4] + rec[5] * rec[5])
    )
    return (disp, rec, total[6] / count - norm_rec)


def solution(mesh):
    in_specs = (
        P(None, "slab", "plane", None),
        P(None, "slab", "plane", None),
        P("slab", "plane", None),
        P(None, "slab", "plane", None),
        P("slab", "plane"),
        P("slab", "plane", None),
    )
    out_specs = (
        P(None, "slab", "plane", None),
        P(None, "slab", "plane", None),
        P("slab", "plane", None),
    )
    return jax.shard_map(body, mesh=mesh, in_specs=in_specs, out_specs=out_specs, check_vma=False)
```

profile of v0, /device:TPU:0, one launch (start us, length us, event | category | flops | bytes accessed | tf_op | source)
XLA Modules:
  0.0 112.8 jit_solution(10212102468267472346)
XLA Ops:
  1.4 2.3 %collective-permute-start = (f32[3,1,8,128]{3,2,1,0:T(8,128)S(1)}, f32[3,1,8,128]{3,2,1,0:T(8,128)S(1)}, u32[]{:S(2)}, u32[]{:S(2)}) collective-permute-start(f32[3,1,8,128]{3,2,1,0:T(8,128)S(1)} %get-tuple-element.37), channel_id=1, source_target_pairs={{0,8},{8,16},{16,24},{1,9},{9,17},{17,25},{2,10},{10,18},{18,26},{... | collective-permute-start | bytes 36872 | tf_op jit(solution)/shard_map/ppermute | solution.py:18
  6.8 2.2 %collective-permute-done.1 = f32[3,1,8,128]{3,2,1,0:T(8,128)S(1)} collective-permute-done((f32[3,1,8,128]{3,2,1,0:T(8,128)S(1)}, f32[3,1,8,128]{3,2,1,0:T(8,128)S(1)}, u32[]{:S(2)}, u32[]{:S(2)}) %collective-permute-start.1) | collective-permute-done | bytes 12320 | tf_op jit(solution)/shard_map/ppermute | solution.py:21
  9.0 3.4 %collective-permute-start.2 = (f32[3,10,1,128]{3,2,1,0:T(1,128)S(1)}, f32[3,10,1,128]{3,2,1,0:T(1,128)S(1)}, u32[]{:S(2)}, u32[]{:S(2)}) collective-permute-start(f32[3,10,1,128]{3,2,1,0:T(1,128)S(1)} %get-tuple-element.34), channel_id=1, source_target_pairs={{0,1},{1,2},{2,3},{3,4},{4,5},{5,6},{6,7},{8,9},{9,10},{10,11},{11... | collective-permute-start | bytes 46088 | tf_op jit(solution)/shard_map/ppermute | solution.py:18
  13.8 4.2 %collective-permute-done.3 = f32[3,10,1,128]{3,2,1,0:T(1,128)S(1)} collective-permute-done((f32[3,10,1,128]{3,2,1,0:T(1,128)S(1)}, f32[3,10,1,128]{3,2,1,0:T(1,128)S(1)}, u32[]{:S(2)}, u32[]{:S(2)}) %collective-permute-start.3) | collective-permute-done | bytes 15392 | tf_op jit(solution)/shard_map/ppermute | solution.py:21
  19.3 2.9 %collective-permute-start.4 = (f32[3,1,16,128]{3,2,1,0:T(8,128)S(1)}, f32[3,1,16,128]{3,2,1,0:T(8,128)S(1)}, u32[]{:S(2)}, u32[]{:S(2)}) collective-permute-start(f32[3,1,16,128]{3,2,1,0:T(8,128)S(1)} %get-tuple-element.30), channel_id=1, source_target_pairs={{0,8},{8,16},{16,24},{1,9},{9,17},{17,25},{2,10},{10,18},{18,26},{... | collective-permute-start | bytes 73736 | tf_op jit(solution)/shard_map/ppermute | solution.py:18
  23.6 3.1 %collective-permute-done.5 = f32[3,1,16,128]{3,2,1,0:T(8,128)S(1)} collective-permute-done((f32[3,1,16,128]{3,2,1,0:T(8,128)S(1)}, f32[3,1,16,128]{3,2,1,0:T(8,128)S(1)}, u32[]{:S(2)}, u32[]{:S(2)}) %collective-permute-start.5) | collective-permute-done | bytes 24608 | tf_op jit(solution)/shard_map/ppermute | solution.py:21
  26.7 4.4 %collective-permute-start.6 = (f32[3,18,1,128]{3,2,1,0:T(1,128)S(1)}, f32[3,18,1,128]{3,2,1,0:T(1,128)S(1)}, u32[]{:S(2)}, u32[]{:S(2)}) collective-permute-start(f32[3,18,1,128]{3,2,1,0:T(1,128)S(1)} %get-tuple-element.22), channel_id=1, source_target_pairs={{0,1},{1,2},{2,3},{3,4},{4,5},{5,6},{6,7},{8,9},{9,10},{10,11},{11... | collective-permute-start | bytes 82952 | tf_op jit(solution)/shard_map/ppermute | solution.py:18
  32.6 4.2 %collective-permute-done.7 = f32[3,18,1,128]{3,2,1,0:T(1,128)S(1)} collective-permute-done((f32[3,18,1,128]{3,2,1,0:T(1,128)S(1)}, f32[3,18,1,128]{3,2,1,0:T(1,128)S(1)}, u32[]{:S(2)}, u32[]{:S(2)}) %collective-permute-start.7) | collective-permute-done | bytes 27680 | tf_op jit(solution)/shard_map/ppermute | solution.py:21
  38.6 3.0 %collective-permute-start.8 = (f32[3,1,16,128]{3,2,1,0:T(8,128)S(1)}, f32[3,1,16,128]{3,2,1,0:T(8,128)S(1)}, u32[]{:S(2)}, u32[]{:S(2)}) collective-permute-start(f32[3,1,16,128]{3,2,1,0:T(8,128)S(1)} %get-tuple-element.28), channel_id=1, source_target_pairs={{0,8},{8,16},{16,24},{1,9},{9,17},{17,25},{2,10},{10,18},{18,26},{... | collective-permute-start | bytes 73736 | tf_op jit(solution)/shard_map/ppermute | solution.py:18
  42.9 2.7 %collective-permute-done.9 = f32[3,1,16,128]{3,2,1,0:T(8,128)S(1)} collective-permute-done((f32[3,1,16,128]{3,2,1,0:T(8,128)S(1)}, f32[3,1,16,128]{3,2,1,0:T(8,128)S(1)}, u32[]{:S(2)}, u32[]{:S(2)}) %collective-permute-start.9) | collective-permute-done | bytes 24608 | tf_op jit(solution)/shard_map/ppermute | solution.py:21
  45.7 3.4 %collective-permute-start.10 = (f32[3,18,1,128]{3,2,1,0:T(1,128)S(1)}, f32[3,18,1,128]{3,2,1,0:T(1,128)S(1)}, u32[]{:S(2)}, u32[]{:S(2)}) collective-permute-start(f32[3,18,1,128]{3,2,1,0:T(1,128)S(1)} %get-tuple-element.20), channel_id=1, source_target_pairs={{0,1},{1,2},{2,3},{3,4},{4,5},{5,6},{6,7},{8,9},{9,10},{10,11},{11... | collective-permute-start | bytes 82952 | tf_op jit(solution)/shard_map/ppermute | solution.py:18
  50.6 4.2 %collective-permute-done.11 = f32[3,18,1,128]{3,2,1,0:T(1,128)S(1)} collective-permute-done((f32[3,18,1,128]{3,2,1,0:T(1,128)S(1)}, f32[3,18,1,128]{3,2,1,0:T(1,128)S(1)}, u32[]{:S(2)}, u32[]{:S(2)}) %collective-permute-start.11) | collective-permute-done | bytes 27680 | tf_op jit(solution)/shard_map/ppermute | solution.py:21
  55.6 3.0 %collective-permute-start.12 = (f32[3,1,16,128]{3,2,1,0:T(8,128)S(1)}, f32[3,1,16,128]{3,2,1,0:T(8,128)S(1)}, u32[]{:S(2)}, u32[]{:S(2)}) collective-permute-start(f32[3,1,16,128]{3,2,1,0:T(8,128)S(1)} %get-tuple-element.26), channel_id=1, source_target_pairs={{0,8},{8,16},{16,24},{1,9},{9,17},{17,25},{2,10},{10,18},{18,26},{... | collective-permute-start | bytes 73736 | tf_op jit(solution)/shard_map/ppermute | solution.py:18
  60.0 2.7 %collective-permute-done.13 = f32[3,1,16,128]{3,2,1,0:T(8,128)S(1)} collective-permute-done((f32[3,1,16,128]{3,2,1,0:T(8,128)S(1)}, f32[3,1,16,128]{3,2,1,0:T(8,128)S(1)}, u32[]{:S(2)}, u32[]{:S(2)}) %collective-permute-start.13) | collective-permute-done | bytes 24608 | tf_op jit(solution)/shard_map/ppermute | solution.py:21
  62.7 4.4 %collective-permute-start.14 = (f32[3,18,1,128]{3,2,1,0:T(1,128)S(1)}, f32[3,18,1,128]{3,2,1,0:T(1,128)S(1)}, u32[]{:S(2)}, u32[]{:S(2)}) collective-permute-start(f32[3,18,1,128]{3,2,1,0:T(1,128)S(1)} %get-tuple-element.18), channel_id=1, source_target_pairs={{0,1},{1,2},{2,3},{3,4},{4,5},{5,6},{6,7},{8,9},{9,10},{10,11},{11... | collective-permute-start | bytes 82952 | tf_op jit(solution)/shard_map/ppermute | solution.py:18
  68.6 4.2 %collective-permute-done.15 = f32[3,18,1,128]{3,2,1,0:T(1,128)S(1)} collective-permute-done((f32[3,18,1,128]{3,2,1,0:T(1,128)S(1)}, f32[3,18,1,128]{3,2,1,0:T(1,128)S(1)}, u32[]{:S(2)}, u32[]{:S(2)}) %collective-permute-start.15) | collective-permute-done | bytes 27680 | tf_op jit(solution)/shard_map/ppermute | solution.py:21
  73.6 3.0 %collective-permute-start.16 = (f32[3,1,16,128]{3,2,1,0:T(8,128)S(1)}, f32[3,1,16,128]{3,2,1,0:T(8,128)S(1)}, u32[]{:S(2)}, u32[]{:S(2)}) collective-permute-start(f32[3,1,16,128]{3,2,1,0:T(8,128)S(1)} %get-tuple-element.24), channel_id=1, source_target_pairs={{0,8},{8,16},{16,24},{1,9},{9,17},{17,25},{2,10},{10,18},{18,26},{... | collective-permute-start | bytes 73736 | tf_op jit(solution)/shard_map/ppermute | solution.py:18
  78.0 2.7 %collective-permute-done.17 = f32[3,1,16,128]{3,2,1,0:T(8,128)S(1)} collective-permute-done((f32[3,1,16,128]{3,2,1,0:T(8,128)S(1)}, f32[3,1,16,128]{3,2,1,0:T(8,128)S(1)}, u32[]{:S(2)}, u32[]{:S(2)}) %collective-permute-start.17) | collective-permute-done | bytes 24608 | tf_op jit(solution)/shard_map/ppermute | solution.py:21
  80.8 3.4 %collective-permute-start.18 = (f32[3,18,1,128]{3,2,1,0:T(1,128)S(1)}, f32[3,18,1,128]{3,2,1,0:T(1,128)S(1)}, u32[]{:S(2)}, u32[]{:S(2)}) collective-permute-start(f32[3,18,1,128]{3,2,1,0:T(1,128)S(1)} %get-tuple-element.16), channel_id=1, source_target_pairs={{0,1},{1,2},{2,3},{3,4},{4,5},{5,6},{6,7},{8,9},{9,10},{10,11},{11... | collective-permute-start | bytes 82952 | tf_op jit(solution)/shard_map/ppermute | solution.py:18
  85.7 4.2 %collective-permute-done.19 = f32[3,18,1,128]{3,2,1,0:T(1,128)S(1)} collective-permute-done((f32[3,18,1,128]{3,2,1,0:T(1,128)S(1)}, f32[3,18,1,128]{3,2,1,0:T(1,128)S(1)}, u32[]{:S(2)}, u32[]{:S(2)}) %collective-permute-start.19) | collective-permute-done | bytes 27680 | tf_op jit(solution)/shard_map/ppermute | solution.py:21
  91.4 3.0 %collective-permute-start.20 = (f32[4,1,16,128]{3,2,1,0:T(8,128)S(1)}, f32[4,1,16,128]{3,2,1,0:T(8,128)S(1)}, u32[]{:S(2)}, u32[]{:S(2)}) collective-permute-start(f32[4,1,16,128]{3,2,1,0:T(8,128)S(1)} %get-tuple-element.14), channel_id=1, source_target_pairs={{0,8},{8,16},{16,24},{1,9},{9,17},{17,25},{2,10},{10,18},{18,26},{... | collective-permute-start | bytes 98312 | tf_op jit(solution)/shard_map/ppermute | solution.py:18
  95.8 2.7 %collective-permute-done.21 = f32[4,1,16,128]{3,2,1,0:T(8,128)S(1)} collective-permute-done((f32[4,1,16,128]{3,2,1,0:T(8,128)S(1)}, f32[4,1,16,128]{3,2,1,0:T(8,128)S(1)}, u32[]{:S(2)}, u32[]{:S(2)}) %collective-permute-start.21) | collective-permute-done | bytes 32800 | tf_op jit(solution)/shard_map/ppermute | solution.py:21
  98.6 4.4 %collective-permute-start.22 = (f32[4,18,1,128]{3,2,1,0:T(1,128)S(1)}, f32[4,18,1,128]{3,2,1,0:T(1,128)S(1)}, u32[]{:S(2)}, u32[]{:S(2)}) collective-permute-start(f32[4,18,1,128]{3,2,1,0:T(1,128)S(1)} %get-tuple-element.12), channel_id=1, source_target_pairs={{0,1},{1,2},{2,3},{3,4},{4,5},{5,6},{6,7},{8,9},{9,10},{10,11},{11... | collective-permute-start | bytes 110600 | tf_op jit(solution)/shard_map/ppermute | solution.py:18
  104.5 4.2 %collective-permute-done.23 = f32[4,18,1,128]{3,2,1,0:T(1,128)S(1)} collective-permute-done((f32[4,18,1,128]{3,2,1,0:T(1,128)S(1)}, f32[4,18,1,128]{3,2,1,0:T(1,128)S(1)}, u32[]{:S(2)}, u32[]{:S(2)}) %collective-permute-start.23) | collective-permute-done | bytes 36896 | tf_op jit(solution)/shard_map/ppermute | solution.py:21
  (105 shorter events, 29.4 us)
Async XLA Ops:
  1.4 4.5 %collective-permute-start = (f32[3,1,8,128]{3,2,1,0:T(8,128)S(1)}, f32[3,1,8,128]{3,2,1,0:T(8,128)S(1)}, u32[]{:S(2)}, u32[]{:S(2)}) collective-permute-start(f32[3,1,8,128]{3,2,1,0:T(8,128)S(1)} %get-tuple-element.37), channel_id=1, source_target_pairs={{0,8},{8,16},{16,24},{1,9},{9,17},{17,25},{2,10},{10,18},{18,26},{... | collective-permute-start | bytes 36872 | tf_op jit(solution)/shard_map/ppermute | solution.py:18
  3.8 5.2 %collective-permute-start.1 = (f32[3,1,8,128]{3,2,1,0:T(8,128)S(1)}, f32[3,1,8,128]{3,2,1,0:T(8,128)S(1)}, u32[]{:S(2)}, u32[]{:S(2)}) collective-permute-start(f32[3,1,8,128]{3,2,1,0:T(8,128)S(1)} %get-tuple-element.36), channel_id=1, source_target_pairs={{8,0},{16,8},{24,16},{9,1},{17,9},{25,17},{10,2},{18,10},{26,18},{... | collective-permute-start | bytes 36872 | tf_op jit(solution)/shard_map/ppermute | solution.py:21
  9.0 4.8 %collective-permute-start.2 = (f32[3,10,1,128]{3,2,1,0:T(1,128)S(1)}, f32[3,10,1,128]{3,2,1,0:T(1,128)S(1)}, u32[]{:S(2)}, u32[]{:S(2)}) collective-permute-start(f32[3,10,1,128]{3,2,1,0:T(1,128)S(1)} %get-tuple-element.34), channel_id=1, source_target_pairs={{0,1},{1,2},{2,3},{3,4},{4,5},{5,6},{6,7},{8,9},{9,10},{10,11},{11... | collective-permute-start | bytes 46088 | tf_op jit(solution)/shard_map/ppermute | solution.py:18
  12.4 5.6 %collective-permute-start.3 = (f32[3,10,1,128]{3,2,1,0:T(1,128)S(1)}, f32[3,10,1,128]{3,2,1,0:T(1,128)S(1)}, u32[]{:S(2)}, u32[]{:S(2)}) collective-permute-start(f32[3,10,1,128]{3,2,1,0:T(1,128)S(1)} %get-tuple-element.35), channel_id=1, source_target_pairs={{1,0},{2,1},{3,2},{4,3},{5,4},{6,5},{7,6},{9,8},{10,9},{11,10},{12... | collective-permute-start | bytes 46088 | tf_op jit(solution)/shard_map/ppermute | solution.py:21
  19.3 4.3 %collective-permute-start.4 = (f32[3,1,16,128]{3,2,1,0:T(8,128)S(1)}, f32[3,1,16,128]{3,2,1,0:T(8,128)S(1)}, u32[]{:S(2)}, u32[]{:S(2)}) collective-permute-start(f32[3,1,16,128]{3,2,1,0:T(8,128)S(1)} %get-tuple-element.30), channel_id=1, source_target_pairs={{0,8},{8,16},{16,24},{1,9},{9,17},{17,25},{2,10},{10,18},{18,26},{... | collective-permute-start | bytes 73736 | tf_op jit(solution)/shard_map/ppermute | solution.py:18
  22.3 4.4 %collective-permute-start.5 = (f32[3,1,16,128]{3,2,1,0:T(8,128)S(1)}, f32[3,1,16,128]{3,2,1,0:T(8,128)S(1)}, u32[]{:S(2)}, u32[]{:S(2)}) collective-permute-start(f32[3,1,16,128]{3,2,1,0:T(8,128)S(1)} %get-tuple-element.31), channel_id=1, source_target_pairs={{8,0},{16,8},{24,16},{9,1},{17,9},{25,17},{10,2},{18,10},{26,18},{... | collective-permute-start | bytes 73736 | tf_op jit(solution)/shard_map/ppermute | solution.py:21
  26.7 5.9 %collective-permute-start.6 = (f32[3,18,1,128]{3,2,1,0:T(1,128)S(1)}, f32[3,18,1,128]{3,2,1,0:T(1,128)S(1)}, u32[]{:S(2)}, u32[]{:S(2)}) collective-permute-start(f32[3,18,1,128]{3,2,1,0:T(1,128)S(1)} %get-tuple-element.22), channel_id=1, source_target_pairs={{0,1},{1,2},{2,3},{3,4},{4,5},{5,6},{6,7},{8,9},{9,10},{10,11},{11... | collective-permute-start | bytes 82952 | tf_op jit(solution)/shard_map/ppermute | solution.py:18
  31.1 5.8 %collective-permute-start.7 = (f32[3,18,1,128]{3,2,1,0:T(1,128)S(1)}, f32[3,18,1,128]{3,2,1,0:T(1,128)S(1)}, u32[]{:S(2)}, u32[]{:S(2)}) collective-permute-start(f32[3,18,1,128]{3,2,1,0:T(1,128)S(1)} %get-tuple-element.23), channel_id=1, source_target_pairs={{1,0},{2,1},{3,2},{4,3},{5,4},{6,5},{7,6},{9,8},{10,9},{11,10},{12... | collective-permute-start | bytes 82952 | tf_op jit(solution)/shard_map/ppermute | solution.py:21
  38.6 4.4 %collective-permute-start.8 = (f32[3,1,16,128]{3,2,1,0:T(8,128)S(1)}, f32[3,1,16,128]{3,2,1,0:T(8,128)S(1)}, u32[]{:S(2)}, u32[]{:S(2)}) collective-permute-start(f32[3,1,16,128]{3,2,1,0:T(8,128)S(1)} %get-tuple-element.28), channel_id=1, source_target_pairs={{0,8},{8,16},{16,24},{1,9},{9,17},{17,25},{2,10},{10,18},{18,26},{... | collective-permute-start | bytes 73736 | tf_op jit(solution)/shard_map/ppermute | solution.py:18
  41.6 4.0 %collective-permute-start.9 = (f32[3,1,16,128]{3,2,1,0:T(8,128)S(1)}, f32[3,1,16,128]{3,2,1,0:T(8,128)S(1)}, u32[]{:S(2)}, u32[]{:S(2)}) collective-permute-start(f32[3,1,16,128]{3,2,1,0:T(8,128)S(1)} %get-tuple-element.29), channel_id=1, source_target_pairs={{8,0},{16,8},{24,16},{9,1},{17,9},{25,17},{10,2},{18,10},{26,18},{... | collective-permute-start | bytes 73736 | tf_op jit(solution)/shard_map/ppermute | solution.py:21
  45.7 4.9 %collective-permute-start.10 = (f32[3,18,1,128]{3,2,1,0:T(1,128)S(1)}, f32[3,18,1,128]{3,2,1,0:T(1,128)S(1)}, u32[]{:S(2)}, u32[]{:S(2)}) collective-permute-start(f32[3,18,1,128]{3,2,1,0:T(1,128)S(1)} %get-tuple-element.20), channel_id=1, source_target_pairs={{0,1},{1,2},{2,3},{3,4},{4,5},{5,6},{6,7},{8,9},{9,10},{10,11},{11... | collective-permute-start | bytes 82952 | tf_op jit(solution)/shard_map/ppermute | solution.py:18
  49.1 5.8 %collective-permute-start.11 = (f32[3,18,1,128]{3,2,1,0:T(1,128)S(1)}, f32[3,18,1,128]{3,2,1,0:T(1,128)S(1)}, u32[]{:S(2)}, u32[]{:S(2)}) collective-permute-start(f32[3,18,1,128]{3,2,1,0:T(1,128)S(1)} %get-tuple-element.21), channel_id=1, source_target_pairs={{1,0},{2,1},{3,2},{4,3},{5,4},{6,5},{7,6},{9,8},{10,9},{11,10},{12... | collective-permute-start | bytes 82952 | tf_op jit(solution)/shard_map/ppermute | solution.py:21
  55.6 4.4 %collective-permute-start.12 = (f32[3,1,16,128]{3,2,1,0:T(8,128)S(1)}, f32[3,1,16,128]{3,2,1,0:T(8,128)S(1)}, u32[]{:S(2)}, u32[]{:S(2)}) collective-permute-start(f32[3,1,16,128]{3,2,1,0:T(8,128)S(1)} %get-tuple-element.26), channel_id=1, source_target_pairs={{0,8},{8,16},{16,24},{1,9},{9,17},{17,25},{2,10},{10,18},{18,26},{... | collective-permute-start | bytes 73736 | tf_op jit(solution)/shard_map/ppermute | solution.py:18
  58.6 4.0 %collective-permute-start.13 = (f32[3,1,16,128]{3,2,1,0:T(8,128)S(1)}, f32[3,1,16,128]{3,2,1,0:T(8,128)S(1)}, u32[]{:S(2)}, u32[]{:S(2)}) collective-permute-start(f32[3,1,16,128]{3,2,1,0:T(8,128)S(1)} %get-tuple-element.27), channel_id=1, source_target_pairs={{8,0},{16,8},{24,16},{9,1},{17,9},{25,17},{10,2},{18,10},{26,18},{... | collective-permute-start | bytes 73736 | tf_op jit(solution)/shard_map/ppermute | solution.py:21
  62.7 5.9 %collective-permute-start.14 = (f32[3,18,1,128]{3,2,1,0:T(1,128)S(1)}, f32[3,18,1,128]{3,2,1,0:T(1,128)S(1)}, u32[]{:S(2)}, u32[]{:S(2)}) collective-permute-start(f32[3,18,1,128]{3,2,1,0:T(1,128)S(1)} %get-tuple-element.18), channel_id=1, source_target_pairs={{0,1},{1,2},{2,3},{3,4},{4,5},{5,6},{6,7},{8,9},{9,10},{10,11},{11... | collective-permute-start | bytes 82952 | tf_op jit(solution)/shard_map/ppermute | solution.py:18
  67.1 5.8 %collective-permute-start.15 = (f32[3,18,1,128]{3,2,1,0:T(1,128)S(1)}, f32[3,18,1,128]{3,2,1,0:T(1,128)S(1)}, u32[]{:S(2)}, u32[]{:S(2)}) collective-permute-start(f32[3,18,1,128]{3,2,1,0:T(1,128)S(1)} %get-tuple-element.19), channel_id=1, source_target_pairs={{1,0},{2,1},{3,2},{4,3},{5,4},{6,5},{7,6},{9,8},{10,9},{11,10},{12... | collective-permute-start | bytes 82952 | tf_op jit(solution)/shard_map/ppermute | solution.py:21
  73.6 4.4 %collective-permute-start.16 = (f32[3,1,16,128]{3,2,1,0:T(8,128)S(1)}, f32[3,1,16,128]{3,2,1,0:T(8,128)S(1)}, u32[]{:S(2)}, u32[]{:S(2)}) collective-permute-start(f32[3,1,16,128]{3,2,1,0:T(8,128)S(1)} %get-tuple-element.24), channel_id=1, source_target_pairs={{0,8},{8,16},{16,24},{1,9},{9,17},{17,25},{2,10},{10,18},{18,26},{... | collective-permute-start | bytes 73736 | tf_op jit(solution)/shard_map/ppermute | solution.py:18
  76.7 4.0 %collective-permute-start.17 = (f32[3,1,16,128]{3,2,1,0:T(8,128)S(1)}, f32[3,1,16,128]{3,2,1,0:T(8,128)S(1)}, u32[]{:S(2)}, u32[]{:S(2)}) collective-permute-start(f32[3,1,16,128]{3,2,1,0:T(8,128)S(1)} %get-tuple-element.25), channel_id=1, source_target_pairs={{8,0},{16,8},{24,16},{9,1},{17,9},{25,17},{10,2},{18,10},{26,18},{... | collective-permute-start | bytes 73736 | tf_op jit(solution)/shard_map/ppermute | solution.py:21
  80.8 4.9 %collective-permute-start.18 = (f32[3,18,1,128]{3,2,1,0:T(1,128)S(1)}, f32[3,18,1,128]{3,2,1,0:T(1,128)S(1)}, u32[]{:S(2)}, u32[]{:S(2)}) collective-permute-start(f32[3,18,1,128]{3,2,1,0:T(1,128)S(1)} %get-tuple-element.16), channel_id=1, source_target_pairs={{0,1},{1,2},{2,3},{3,4},{4,5},{5,6},{6,7},{8,9},{9,10},{10,11},{11... | collective-permute-start | bytes 82952 | tf_op jit(solution)/shard_map/ppermute | solution.py:18
  84.2 5.8 %collective-permute-start.19 = (f32[3,18,1,128]{3,2,1,0:T(1,128)S(1)}, f32[3,18,1,128]{3,2,1,0:T(1,128)S(1)}, u32[]{:S(2)}, u32[]{:S(2)}) collective-permute-start(f32[3,18,1,128]{3,2,1,0:T(1,128)S(1)} %get-tuple-element.17), channel_id=1, source_target_pairs={{1,0},{2,1},{3,2},{4,3},{5,4},{6,5},{7,6},{9,8},{10,9},{11,10},{12... | collective-permute-start | bytes 82952 | tf_op jit(solution)/shard_map/ppermute | solution.py:21
  91.4 4.3 %collective-permute-start.20 = (f32[4,1,16,128]{3,2,1,0:T(8,128)S(1)}, f32[4,1,16,128]{3,2,1,0:T(8,128)S(1)}, u32[]{:S(2)}, u32[]{:S(2)}) collective-permute-start(f32[4,1,16,128]{3,2,1,0:T(8,128)S(1)} %get-tuple-element.14), channel_id=1, source_target_pairs={{0,8},{8,16},{16,24},{1,9},{9,17},{17,25},{2,10},{10,18},{18,26},{... | collective-permute-start | bytes 98312 | tf_op jit(solution)/shard_map/ppermute | solution.py:18
  94.4 4.0 %collective-permute-start.21 = (f32[4,1,16,128]{3,2,1,0:T(8,128)S(1)}, f32[4,1,16,128]{3,2,1,0:T(8,128)S(1)}, u32[]{:S(2)}, u32[]{:S(2)}) collective-permute-start(f32[4,1,16,128]{3,2,1,0:T(8,128)S(1)} %get-tuple-element.15), channel_id=1, source_target_pairs={{8,0},{16,8},{24,16},{9,1},{17,9},{25,17},{10,2},{18,10},{26,18},{... | collective-permute-start | bytes 98312 | tf_op jit(solution)/shard_map/ppermute | solution.py:21
  98.6 6.0 %collective-permute-start.22 = (f32[4,18,1,128]{3,2,1,0:T(1,128)S(1)}, f32[4,18,1,128]{3,2,1,0:T(1,128)S(1)}, u32[]{:S(2)}, u32[]{:S(2)}) collective-permute-start(f32[4,18,1,128]{3,2,1,0:T(1,128)S(1)} %get-tuple-element.12), channel_id=1, source_target_pairs={{0,1},{1,2},{2,3},{3,4},{4,5},{5,6},{6,7},{8,9},{9,10},{10,11},{11... | collective-permute-start | bytes 110600 | tf_op jit(solution)/shard_map/ppermute | solution.py:18
  102.9 5.9 %collective-permute-start.23 = (f32[4,18,1,128]{3,2,1,0:T(1,128)S(1)}, f32[4,18,1,128]{3,2,1,0:T(1,128)S(1)}, u32[]{:S(2)}, u32[]{:S(2)}) collective-permute-start(f32[4,18,1,128]{3,2,1,0:T(1,128)S(1)} %get-tuple-element.13), channel_id=1, source_target_pairs={{1,0},{2,1},{3,2},{4,3},{5,4},{6,5},{7,6},{9,8},{10,9},{11,10},{12... | collective-permute-start | bytes 110600 | tf_op jit(solution)/shard_map/ppermute | solution.py:21
  (6 other events, 50.5 us)
where the time goes:
time: 114 us; the launch traced here: 113 us
  starting transfers between devices  56.1 us (49%)
  waiting for transfers between devices  42.4 us (37%)
  other arithmetic  8.66 us (8%)
  local copies, waits for them, and re-layouts  4.31 us (4%)
  between operations  1.27 us (1%)
    ppermute x12, waiting for transfers between devices, extended(): lax.ppermute(lax.slice_in_dim(block, 0, width, axis=dim), axis, backward)  41.4 us
    ppermute x12, starting transfers between devices, extended(): lax.ppermute(lax.slice_in_dim(block, block.shape[dim] - width, None, axis...  40.6 us
    ppermute x12, starting transfers between devices, extended(): lax.ppermute(lax.slice_in_dim(block, 0, width, axis=dim), axis, backward)  15.5 us
    unnamed x14, local copies, waits for them, and re-layouts  2.3 us
  transfers between devices with their start and end apart: 24, of which 18 were waited for; matrix products, arithmetic and copies ran while one was open for 2% of the time, Pallas kernels for 0%

commit v1 on v0

v1 whole, which is shorter than its diff:
```python
import functools

import jax
import jax.numpy as jnp
from jax import lax
from jax.experimental import pallas as pl
from jax.experimental.pallas import tpu as pltpu
from jax.sharding import PartitionSpec as P

DEGREE = 4
THETA = 4.5
DELTA_C = 3.5
SIGMA = THETA / DELTA_C
MESH = pl.DeviceIdType.MESH
OFF = 8
SIDES = ((0, 1), (0, -1), (1, 1), (1, -1), (-1, 1), (-1, -1), (1, 0), (-1, 0))
LOW_SIDES = ((0, 1), (1, 1), (1, 0))


def edge(step, first, count):
    if step > 0:
        return pl.ds(first + count - 1, 1), pl.ds(first - 1, 1)
    if step < 0:
        return pl.ds(first, 1), pl.ds(first + count, 1)
    return pl.ds(first, count), pl.ds(first, count)


def box_z(x):
    lane = lax.broadcasted_iota(jnp.int32, x.shape, x.ndim - 1)
    depth = x.shape[-1]
    below = jnp.where(lane == 0, 0.0, pltpu.roll(x, 1, x.ndim - 1))
    above = jnp.where(lane == depth - 1, 0.0, pltpu.roll(x, depth - 1, x.ndim - 1))
    return x + below + above


def next_z(x):
    return pltpu.roll(x, x.shape[-1] - 1, x.ndim - 1)


def previous_z(x):
    return pltpu.roll(x, 1, x.ndim - 1)


def smooth(sizes, refs):
    nx, ny, depth, kx, ky, slabs, planes = sizes
    (start_hbm, load_hbm, shift_hbm, coarse_hbm, agg_hbm, cons_hbm,
     start, load, shift, table, agg, cons, fields, resid,
     in_sem, send_sem, recv_sem) = refs
    slab = lax.axis_index("slab")
    plane = lax.axis_index("plane")

    def exists(step_x, step_y):
        x, y = slab + step_x, plane + step_y
        return (x >= 0) & (x < slabs) & (y >= 0) & (y < planes)

    loads = [
        pltpu.make_async_copy(coarse_hbm, table.at[:, pl.ds(1, kx), pl.ds(0, ky)], in_sem.at[0]),
        pltpu.make_async_copy(agg_hbm, agg, in_sem.at[1]),
        pltpu.make_async_copy(start_hbm, start, in_sem.at[2]),
        pltpu.make_async_copy(cons_hbm, cons.at[pl.ds(1, nx), pl.ds(OFF, ny)], in_sem.at[3]),
        pltpu.make_async_copy(load_hbm, load, in_sem.at[4]),
        pltpu.make_async_copy(shift_hbm, shift, in_sem.at[5]),
    ]
    for copy in loads:
        copy.start()

    zero_table = jnp.zeros((3, 8, depth), jnp.float32)
    for a in range(kx + 2):
        table[:, a, ky:ky + 8, :] = zero_table
    table[:, 0, 0:ky, :] = zero_table
    table[:, kx + 1, 0:ky, :] = zero_table

    barrier = pltpu.get_barrier_semaphore()
    for step_x, step_y in SIDES:
        @pl.when(exists(step_x, step_y))
        def _():
            pl.semaphore_signal(
                barrier, inc=1, device_id=(slab + step_x, plane + step_y), device_id_type=MESH
            )

    zero_row = jnp.zeros((nx + 2, depth), jnp.float32)
    for step_x, step_y in ((0, 1), (0, -1), (1, 0), (-1, 0)):
        @pl.when(jnp.logical_not(exists(-step_x, -step_y)))
        def _():
            for phase in range(DEGREE + 1):
                for c in range(3):
                    if step_y:
                        row = OFF - 1 if step_y > 0 else OFF + ny
                        for i in range(nx + 2):
                            fields[phase, c, i, row:row + 1, :] = zero_row[0:1]
                    else:
                        i = 0 if step_x > 0 else nx + 1
                        for at in range(0, ny + 16, 8):
                            fields[phase, c, i, at:at + 8, :] = zero_row[0:8]

    near_x = 1 + (slab > 0).astype(jnp.int32) + (slab < slabs - 1).astype(jnp.int32)
    near_y = 1 + (plane > 0).astype(jnp.int32) + (plane < planes - 1).astype(jnp.int32)
    pl.semaphore_wait(barrier, near_x * near_y - 1)

    def remote(source, target, phase, side):
        step_x, step_y = SIDES[side]
        return pltpu.make_async_remote_copy(
            src_ref=source, dst_ref=target,
            send_sem=send_sem.at[phase, side], recv_sem=recv_sem.at[phase, side],
            device_id=(slab + step_x, plane + step_y), device_id_type=MESH,
        )

    def start_all(make, phase, sides=SIDES):
        for side, (step_x, step_y) in enumerate(SIDES):
            if (step_x, step_y) in sides:
                @pl.when(exists(step_x, step_y))
                def _():
                    remote(*make(step_x, step_y), phase, side).start()

    def wait_arrived(make, phase, sides=SIDES):
        for side, (step_x, step_y) in enumerate(SIDES):
            if (step_x, step_y) in sides:
                @pl.when(exists(-step_x, -step_y))
                def _():
                    remote(*make(step_x, step_y), phase, side).wait_recv()

    def wait_sent(make, phase, sides=SIDES):
        for side, (step_x, step_y) in enumerate(SIDES):
            if (step_x, step_y) in sides:
                @pl.when(exists(step_x, step_y))
                def _():
                    remote(*make(step_x, step_y), phase, side).wait_send()

    def coarse_edge(step_x, step_y):
        from_x, to_x = edge(step_x, 1, kx)
        from_y, to_y = edge(step_y, 0, ky)
        from_x = pl.ds(from_x.start - 1, from_x.size)
        if step_y > 0:
            to_y = pl.ds(ky + 7, 1)
        return coarse_hbm.at[:, from_x, from_y], table.at[:, to_x, to_y]

    def cons_edge(step_x, step_y):
        from_x, to_x = edge(step_x, 1, nx)
        from_y, to_y = edge(step_y, OFF, ny)
        return (
            cons_hbm.at[pl.ds(from_x.start - 1, from_x.size), pl.ds(from_y.start - OFF, from_y.size)],
            cons.at[to_x, to_y],
        )

    def field_edge(phase):
        def make(step_x, step_y):
            from_x, to_x = edge(step_x, 1, nx)
            from_y, to_y = edge(step_y, OFF, ny)
            return fields.at[phase, :, from_x, from_y], fields.at[phase, :, to_x, to_y]
        return make

    last = DEGREE + 1
    start_all(coarse_edge, last)

    loads[1].wait()
    cols = ky * planes
    whole = agg[...]
    if cols & (cols - 1) == 0:
        row_a = lax.shift_right_logical(whole, cols.bit_length() - 1)
    else:
        row_a = lax.div(whole, cols)
    place = (row_a - (slab * kx - 1)) * (ky + 8)
    col_b = whole - row_a * cols - plane * ky
    place = (place + jnp.where(col_b < 0, ky + 7, col_b)).astype(jnp.float32)
    deep = (kx + 2) * (ky + 8)
    own = lax.broadcasted_iota(jnp.int32, (ny, ny), 0) == lax.broadcasted_iota(jnp.int32, (ny, ny), 1)
    slots = lax.broadcasted_iota(jnp.int32, (ny, deep), 1).astype(jnp.float32)
    picks = []
    for i in range(nx):
        column = jnp.sum(jnp.where(own, place[i:i + 1, :], 0.0), axis=1, keepdims=True)
        picks.append((column == slots).astype(jnp.bfloat16))
    pick = jnp.concatenate(picks, axis=0)
    loads[0].wait()
    loads[2].wait()
    wait_arrived(coarse_edge, last)
    for c in range(3):
        rest = table[c].reshape(deep, depth)
        moved = None
        for _ in range(3):
            part = rest.astype(jnp.bfloat16)
            rest = rest - part.astype(jnp.float32)
            piece = jnp.dot(pick, part, preferred_element_type=jnp.float32)
            moved = piece if moved is None else moved + piece
        fields[0, c, 1:nx + 1, OFF:OFF + ny, :] = start[c] + moved.reshape(nx, ny, depth)

    start_all(field_edge(0), 0)
    start_all(cons_edge, last + 1, LOW_SIDES)
    loads[4].wait()
    loads[5].wait()

    rows = 4
    rho = 1.0 / SIGMA
    for phase in range(DEGREE):
        wait_arrived(field_edge(phase), phase)
        if phase:
            rho_new = 1.0 / (2.0 * SIGMA - rho)
            keep, gain = rho_new * rho, 2.0 * rho_new / DELTA_C
            rho = rho_new

        def chunk(n, carry):
            c = n // (nx // rows)
            first = (n % (nx // rows)) * rows
            span = pl.ds(first, rows + 2)
            along_y = (
                fields[phase, c, span, pl.ds(OFF - 1, ny), :]
                + fields[phase, c, span, pl.ds(OFF, ny), :]
                + fields[phase, c, span, pl.ds(OFF + 1, ny), :]
            )
            boxed = box_z(along_y[:-2] + along_y[1:-1] + along_y[2:])
            centre = fields[phase, c, pl.ds(first + 1, rows), pl.ds(OFF, ny), :]
            here = pl.ds(first, rows)
            applied = (3.0 + shift[here]) * centre - boxed * (1.0 / 3.0)
            if phase == 0:
                left = load[c, here] - applied
                direction = left * (1.0 / THETA)
            else:
                left = resid[c, here] - applied
                direction = keep * centre + gain * left
            inner = (c, pl.ds(first + 1, rows), pl.ds(OFF, ny))
            if phase < DEGREE - 1:
                resid[c, here] = left
            else:
                for earlier in range(DEGREE):
                    direction = direction + fields[(earlier,) + inner]
            fields[(phase + 1,) + inner] = direction
            return carry

        lax.fori_loop(0, 3 * (nx // rows), chunk, 0)
        start_all(field_edge(phase + 1), phase + 1)

    loads[3].wait()
    wait_arrived(cons_edge, last + 1, LOW_SIDES)
    wait_arrived(field_edge(DEGREE), DEGREE)

    def finish():
        wait_sent(coarse_edge, last)
        wait_sent(cons_edge, last + 1, LOW_SIDES)
        for phase in range(DEGREE + 1):
            wait_sent(field_edge(phase), phase)

    return finish


def stresses(sizes, field, cons, disp_out, rec_out, ind_out):
    nx, ny, depth, kx, ky, slabs, planes = sizes
    first_x = lax.axis_index("slab") * nx
    first_y = lax.axis_index("plane") * ny
    total_x, total_y = nx * slabs, ny * planes
    tall = ny + 8
    lane = lax.broadcasted_iota(jnp.int32, (tall, depth), 1)
    node_y = first_y - 1 + lax.broadcasted_iota(jnp.int32, (tall, depth), 0)
    valid_y = (node_y >= 0) & (node_y <= total_y - 2) & (lane <= depth - 2)
    lane = lax.broadcasted_iota(jnp.int32, (ny, depth), 1)
    node_y = first_y + lax.broadcasted_iota(jnp.int32, (ny, depth), 0)

    def half(ok):
        return jnp.where(ok, 0.5, 1.0)

    scale_y = half((node_y >= 1) & (node_y <= total_y - 2)) * half((lane >= 1) & (lane <= depth - 2))

    for c in range(3):
        disp_out[c] = field[c, 1:nx + 1, OFF:OFF + ny, :]

    def corner_sums(c, i):
        low = field[c, i, pl.ds(OFF - 1, tall), :]
        high = field[c, i, pl.ds(OFF, tall), :]
        return low + high, high - low

    def element_row(i):
        grad_x, grad_y, grad_z = [], [], []
        for c in range(3):
            sum_a, diff_a = corner_sums(c, i)
            sum_b, diff_b = corner_sums(c, i + 1)
            gx, gy, gz = sum_b - sum_a, diff_a + diff_b, sum_a + sum_b
            grad_x.append(0.25 * (gx + next_z(gx)))
            grad_y.append(0.25 * (gy + next_z(gy)))
            grad_z.append(0.25 * (next_z(gz) - gz))
        exx, eyy, ezz = grad_x[0], grad_y[1], grad_z[2]
        exy = 0.5 * (grad_y[0] + grad_x[1])
        eyz = 0.5 * (grad_z[1] + grad_y[2])
        ezx = 0.5 * (grad_x[2] + grad_z[0])
        trace = exx + eyy + ezz
        third = trace * (1.0 / 3.0)
        sxx, syy, szz = exx - third, eyy - third, ezz - third
        equiv = (2.0 / 3.0) * (
            sxx * sxx + syy * syy + szz * szz + 2.0 * (exy * exy + eyz * eyz + ezx * ezx)
        )
        visc = cons[i, pl.ds(OFF - 1, tall), :] * jnp.exp(-0.425 * jnp.log(0.01 + 3.0 * equiv))
        twice = 2.0 * visc
        bulk = 4.0 * trace
        sig = [twice * sxx + bulk, twice * syy + bulk, twice * szz + bulk,
               twice * exy, twice * eyz, twice * ezx]
        norm_sq = (
            sig[0] * sig[0] + sig[1] * sig[1] + sig[2] * sig[2]
            + 2.0 * (sig[3] * sig[3] + sig[4] * sig[4] + sig[5] * sig[5])
        )
        node_x = first_x - 1 + i
        valid = valid_y & (node_x >= 0) & (node_x <= total_x - 2)
        summed = []
        for one in sig + [norm_sq]:
            one = jnp.where(valid, one, 0.0)
            one = one[0:ny] + one[1:ny + 1]
            summed.append(one + previous_z(one))
        return tuple(summed)

    def row(i, before):
        after = element_row(i)
        node_x = first_x + i - 1
        inside = ((node_x >= 1) & (node_x <= total_x - 2)).astype(jnp.float32)
        scale = scale_y * (1.0 - 0.5 * inside)
        total = [(a + b) * scale for a, b in zip(before, after)]
        rec = total[:6]
        for n in range(6):
            rec_out[n, i - 1] = rec[n]
        ind_out[i - 1] = total[6] - (
            rec[0] * rec[0] + rec[1] * rec[1] + rec[2] * rec[2]
            + 2.0 * (rec[3] * rec[3] + rec[4] * rec[4] + rec[5] * rec[5])
        )
        return after

    lax.fori_loop(1, nx + 1, row, element_row(0))


def whole_kernel(sizes, *refs):
    inputs, outs, scratch = refs[:6], refs[6:9], refs[9:]
    finish = smooth(sizes, inputs + scratch)
    fields, cons = scratch[6], scratch[5]
    stresses(sizes, fields.at[DEGREE], cons, *outs)
    finish()


def body(sizes, *blocks):
    nx, ny, depth, kx, ky, slabs, planes = sizes
    any_spec = pl.BlockSpec(memory_space=pl.ANY)
    vmem_spec = pl.BlockSpec(memory_space=pltpu.VMEM)
    f32 = jnp.float32
    return pl.pallas_call(
        functools.partial(whole_kernel, sizes),
        out_shape=(
            jax.ShapeDtypeStruct((3, nx, ny, depth), f32),
            jax.ShapeDtypeStruct((6, nx, ny, depth), f32),
            jax.ShapeDtypeStruct((nx, ny, depth), f32),
        ),
        in_specs=[any_spec] * 6,
        out_specs=(vmem_spec,) * 3,
        scratch_shapes=[
            pltpu.VMEM((3, nx, ny, depth), f32),
            pltpu.VMEM((3, nx, ny, depth), f32),
            pltpu.VMEM((nx, ny, depth), f32),
            pltpu.VMEM((3, kx + 2, ky + 8, depth), f32),
            pltpu.VMEM((nx, ny), jnp.int32),
            pltpu.VMEM((nx + 1, ny + 16, depth), f32),
            pltpu.VMEM((DEGREE + 1, 3, nx + 2, ny + 16, depth), f32),
            pltpu.VMEM((3, nx, ny, depth), f32),
            pltpu.SemaphoreType.DMA((6,)),
            pltpu.SemaphoreType.DMA((DEGREE + 3, len(SIDES))),
            pltpu.SemaphoreType.DMA((DEGREE + 3, len(SIDES))),
        ],
        compiler_params=pltpu.CompilerParams(
            collective_id=0, has_side_effects=True, vmem_limit_bytes=32 * 1024 * 1024
        ),
    )(*blocks)


def solution(mesh):
    in_specs = (
        P(None, "slab", "plane", None),
        P(None, "slab", "plane", None),
        P("slab", "plane", None),
        P(None, "slab", "plane", None),
        P("slab", "plane"),
        P("slab", "plane", None),
    )
    out_specs = (
        P(None, "slab", "plane", None),
        P(None, "slab", "plane", None),
        P("slab", "plane", None),
    )
    slabs, planes = mesh.shape["slab"], mesh.shape["plane"]

    def run(start_disp, load, shift, coarse, aggregate, consistency):
        sizes = (
            start_disp.shape[1] // slabs, start_disp.shape[2] // planes, start_disp.shape[3],
            coarse.shape[1] // slabs, coarse.shape[2] // planes, slabs, planes,
        )
        return jax.shard_map(
            functools.partial(body, sizes), mesh=mesh, in_specs=in_specs, out_specs=out_specs,
            check_vma=False,
        )(start_disp, load, shift, coarse, aggregate, consistency)

    return run
```

time: 114 us -> 44.6 us (0.39)
  starting transfers between devices: 56.1 us -> 0 us
  waiting for transfers between devices: 42.4 us -> 0 us
  Pallas kernels: 0 us -> 36 us
  other arithmetic: 8.66 us -> 0 us
  local copies, waits for them, and re-layouts: 4.31 us -> 7.66 us
    ppermute x24 -> x0, starting transfers between devices: 56.1 us -> none  [the longest x12 40.6 us: extended(): lax.ppermute(lax.slice_in_dim(block, block.shape[dim] - width, None, axis...]
    ppermute x24 -> x0, waiting for transfers between devices: 42.4 us -> none  [the longest x12 41.4 us: extended(): lax.ppermute(lax.slice_in_dim(block, 0, width, axis=dim), axis, backward)]
    pallas_call x0 -> x1, Pallas kernels: none -> 36 us  [body(): pl.pallas_call(functools.partial(whole_kernel, sizes), out_shape=(jax.Sha...]
    unnamed x14 -> x15, local copies, waits for them, and re-layouts: 2.3 us -> 7.66 us
    add x17 -> x0, other arithmetic: 3.32 us -> none  [the longest x4 1.63 us: stiff_apply(): along_z = zpad[..., :-2] + zpad[..., 1:-1] + zpad[..., 2:]]
    sub x4 -> x0, other arithmetic: 1.34 us -> none  [the longest x1 0.9 us: body(): return (disp, rec, total[6] / count - norm_rec)]
    mul x6 -> x0, other arithmetic: 1.17 us -> none  [the longest x1 0.46 us: element_stress(): 0.25 * (diff_z[:, :-1, :-1] + diff_z[:, 1:, :-1] + diff_z[:, :-1, 1:] + d...]
  transfers between devices with their start and end apart: 24 -> 0, of which waited for: 18 -> 0; matrix products, arithmetic and copies ran while one was open for 2% -> 0% of each run, Pallas kernels for 0% -> 0%
where the time goes in v1:
time: 44.6 us; the launch traced here: 44.3 us
  Pallas kernels  36 us (81%)
  local copies, waits for them, and re-layouts  7.66 us (17%)
  between operations  0.65 us (1%)
    pallas_call x1, Pallas kernels, body(): pl.pallas_call(functools.partial(whole_kernel, sizes), out_shape=(jax.Sha...  36 us
    unnamed x15, local copies, waits for them, and re-layouts  7.66 us

profile of v1, /device:TPU:0, one launch (start us, length us, event | category | flops | bytes accessed | tf_op | source)
XLA Modules:
  0.0 44.3 jit_solution(15867327927671656749)
XLA Ops:
  0.6 0.0 copy-start
  0.6 1.0 %copy-done = f32[3,16,16,128]{3,2,1,0:T(8,128)S(1)} copy-done((f32[3,16,16,128]{3,2,1,0:T(8,128)S(1)}, f32[3,16,16,128]{3,2,1,0:T(8,128)}, u32[]{:S(2)}) %copy-start) | copy-done | bytes 393240
  1.6 0.0 copy-start.1
  1.6 1.0 %copy-done.1 = f32[3,16,16,128]{3,2,1,0:T(8,128)S(1)} copy-done((f32[3,16,16,128]{3,2,1,0:T(8,128)S(1)}, f32[3,16,16,128]{3,2,1,0:T(8,128)}, u32[]{:S(2)}) %copy-start.1) | copy-done | bytes 393240
  2.6 0.0 copy-start.2
  2.6 0.9 %copy-done.2 = f32[16,16,128]{2,1,0:T(8,128)S(1)} copy-done((f32[16,16,128]{2,1,0:T(8,128)S(1)}, f32[16,16,128]{2,1,0:T(8,128)}, u32[]{:S(2)}) %copy-start.2) | copy-done | bytes 131096
  3.5 0.0 copy-start.3
  3.5 0.9 %copy-done.3 = f32[16,16,128]{2,1,0:T(8,128)S(1)} copy-done((f32[16,16,128]{2,1,0:T(8,128)S(1)}, f32[16,16,128]{2,1,0:T(8,128)}, u32[]{:S(2)}) %copy-start.3) | copy-done | bytes 131096
  4.4 0.0 copy-start.4
  4.4 0.9 %copy-done.4 = f32[3,8,8,128]{3,2,1,0:T(8,128)S(1)} copy-done((f32[3,8,8,128]{3,2,1,0:T(8,128)S(1)}, f32[3,8,8,128]{3,2,1,0:T(8,128)}, u32[]{:S(2)}) %copy-start.4) | copy-done | bytes 98328
  5.3 0.0 copy-start.5
  5.3 0.7 %copy-done.5 = s32[16,16]{1,0:T(8,128)S(1)} copy-done((s32[16,16]{1,0:T(8,128)S(1)}, s32[16,16]{1,0:T(8,128)}, u32[]{:S(2)}) %copy-start.5) | copy-done | bytes 1048
  6.0 36.0 %shard_map.85 = (f32[3,16,16,128]{3,2,1,0:T(8,128)S(1)}, f32[6,16,16,128]{3,2,1,0:T(8,128)S(1)}, f32[16,16,128]{2,1,0:T(8,128)S(1)}) custom-call(f32[3,16,16,128]{3,2,1,0:T(8,128)S(1)} %copy-done, f32[3,16,16,128]{3,2,1,0:T(8,128)S(1)} %copy-done.1, f32[16,16,128]{2,1,0:T(8,128)S(1)} %copy-done.2, f32[3,8,8,128]{3,2,1,0:T(8,128)S(1)} %copy-done.4, ...), custom_call_target="tpu_custom_call" | custom-call | tf_op jit(solution)/shard_map/pallas_call | solution.py:337
  42.0 0.7 %copy.12 = f32[3,16,16,128]{3,2,1,0:T(8,128)} copy(f32[3,16,16,128]{3,2,1,0:T(8,128)S(1)} %get-tuple-element.6) | data formatting | bytes 786432
  42.8 0.9 %copy.13 = f32[6,16,16,128]{3,2,1,0:T(8,128)} copy(f32[6,16,16,128]{3,2,1,0:T(8,128)S(1)} %get-tuple-element.7) | data formatting | bytes 1572864
  43.6 0.7 %copy.14 = f32[16,16,128]{2,1,0:T(8,128)} copy(f32[16,16,128]{2,1,0:T(8,128)S(1)} %get-tuple-element.8) | data formatting | bytes 262144
Async XLA Ops:
  0.6 1.0 %copy-start = (f32[3,16,16,128]{3,2,1,0:T(8,128)S(1)}, f32[3,16,16,128]{3,2,1,0:T(8,128)}, u32[]{:S(2)}) copy-start(f32[3,16,16,128]{3,2,1,0:T(8,128)} %refs_0_.1) | copy-start | bytes 1179652
  1.6 1.0 %copy-start.1 = (f32[3,16,16,128]{3,2,1,0:T(8,128)S(1)}, f32[3,16,16,128]{3,2,1,0:T(8,128)}, u32[]{:S(2)}) copy-start(f32[3,16,16,128]{3,2,1,0:T(8,128)} %refs_1_.1) | copy-start | bytes 1179652
  2.6 0.9 %copy-start.2 = (f32[16,16,128]{2,1,0:T(8,128)S(1)}, f32[16,16,128]{2,1,0:T(8,128)}, u32[]{:S(2)}) copy-start(f32[16,16,128]{2,1,0:T(8,128)} %refs_2_.1) | copy-start | bytes 393220
  3.5 0.9 %copy-start.3 = (f32[16,16,128]{2,1,0:T(8,128)S(1)}, f32[16,16,128]{2,1,0:T(8,128)}, u32[]{:S(2)}) copy-start(f32[16,16,128]{2,1,0:T(8,128)} %refs_5_.1) | copy-start | bytes 393220
  4.4 0.9 %copy-start.4 = (f32[3,8,8,128]{3,2,1,0:T(8,128)S(1)}, f32[3,8,8,128]{3,2,1,0:T(8,128)}, u32[]{:S(2)}) copy-start(f32[3,8,8,128]{3,2,1,0:T(8,128)} %refs_3_.1) | copy-start | bytes 294916
  5.3 0.7 %copy-start.5 = (s32[16,16]{1,0:T(8,128)S(1)}, s32[16,16]{1,0:T(8,128)}, u32[]{:S(2)}) copy-start(s32[16,16]{1,0:T(8,128)} %refs_4_.1) | copy-start | bytes 3076

commit v2 on v1

--- a/solution.py
+++ b/solution.py
@@ -14,6 +14,8 @@
 MESH = pl.DeviceIdType.MESH
 OFF = 8
 SIDES = ((0, 1), (0, -1), (1, 1), (1, -1), (-1, 1), (-1, -1), (1, 0), (-1, 0))
+VMEM_BYTES = 56 * 1024 * 1024
+ROWS_OUT = 4
 LOW_SIDES = ((0, 1), (1, 1), (1, 0))
 
 
@@ -41,11 +43,11 @@
     return pltpu.roll(x, 1, x.ndim - 1)
 
 
-def smooth(sizes, refs):
+def smooth(sizes, *refs):
     nx, ny, depth, kx, ky, slabs, planes = sizes
-    (start_hbm, load_hbm, shift_hbm, coarse_hbm, agg_hbm, cons_hbm,
-     start, load, shift, table, agg, cons, fields, resid,
-     in_sem, send_sem, recv_sem) = refs
+    (start_hbm, load_hbm, shift_hbm, coarse_hbm, agg_hbm, cons_hbm, final, cons,
+     start, load, shift, table, agg, earlier, resid, in_sem, send_sem, recv_sem) = refs
+    fields = [earlier.at[n] for n in range(DEGREE)] + [final]
     slab = lax.axis_index("slab")
     plane = lax.axis_index("plane")
 
@@ -87,11 +89,11 @@
                     if step_y:
                         row = OFF - 1 if step_y > 0 else OFF + ny
                         for i in range(nx + 2):
-                            fields[phase, c, i, row:row + 1, :] = zero_row[0:1]
+                            fields[phase][c, i, row:row + 1, :] = zero_row[0:1]
                     else:
                         i = 0 if step_x > 0 else nx + 1
                         for at in range(0, ny + 16, 8):
-                            fields[phase, c, i, at:at + 8, :] = zero_row[0:8]
+                            fields[phase][c, i, at:at + 8, :] = zero_row[0:8]
 
     near_x = 1 + (slab > 0).astype(jnp.int32) + (slab < slabs - 1).astype(jnp.int32)
     near_y = 1 + (plane > 0).astype(jnp.int32) + (plane < planes - 1).astype(jnp.int32)
@@ -146,7 +148,7 @@
         def make(step_x, step_y):
             from_x, to_x = edge(step_x, 1, nx)
             from_y, to_y = edge(step_y, OFF, ny)
-            return fields.at[phase, :, from_x, from_y], fields.at[phase, :, to_x, to_y]
+            return fields[phase].at[:, from_x, from_y], fields[phase].at[:, to_x, to_y]
         return make
 
     last = DEGREE + 1
@@ -181,7 +183,7 @@
             rest = rest - part.astype(jnp.float32)
             piece = jnp.dot(pick, part, preferred_element_type=jnp.float32)
             moved = piece if moved is None else moved + piece
-        fields[0, c, 1:nx + 1, OFF:OFF + ny, :] = start[c] + moved.reshape(nx, ny, depth)
+        fields[0][c, 1:nx + 1, OFF:OFF + ny, :] = start[c] + moved.reshape(nx, ny, depth)
 
     start_all(field_edge(0), 0)
     start_all(cons_edge, last + 1, LOW_SIDES)
@@ -197,17 +199,17 @@
             keep, gain = rho_new * rho, 2.0 * rho_new / DELTA_C
             rho = rho_new
 
-        def chunk(n, carry):
-            c = n // (nx // rows)
-            first = (n % (nx // rows)) * rows
+        def chunk(at, carry):
+            c = at // (nx // rows)
+            first = (at % (nx // rows)) * rows
             span = pl.ds(first, rows + 2)
             along_y = (
-                fields[phase, c, span, pl.ds(OFF - 1, ny), :]
-                + fields[phase, c, span, pl.ds(OFF, ny), :]
-                + fields[phase, c, span, pl.ds(OFF + 1, ny), :]
+                fields[phase][c, span, pl.ds(OFF - 1, ny), :]
+                + fields[phase][c, span, pl.ds(OFF, ny), :]
+                + fields[phase][c, span, pl.ds(OFF + 1, ny), :]
             )
             boxed = box_z(along_y[:-2] + along_y[1:-1] + along_y[2:])
-            centre = fields[phase, c, pl.ds(first + 1, rows), pl.ds(OFF, ny), :]
+            centre = fields[phase][c, pl.ds(first + 1, rows), pl.ds(OFF, ny), :]
             here = pl.ds(first, rows)
             applied = (3.0 + shift[here]) * centre - boxed * (1.0 / 3.0)
             if phase == 0:
@@ -220,9 +222,9 @@
             if phase < DEGREE - 1:
                 resid[c, here] = left
             else:
-                for earlier in range(DEGREE):
-                    direction = direction + fields[(earlier,) + inner]
-            fields[(phase + 1,) + inner] = direction
+                for n in range(DEGREE):
+                    direction = direction + fields[n][inner]
+            fields[phase + 1][inner] = direction
             return carry
 
         lax.fori_loop(0, 3 * (nx // rows), chunk, 0)
@@ -232,16 +234,13 @@
     wait_arrived(cons_edge, last + 1, LOW_SIDES)
     wait_arrived(field_edge(DEGREE), DEGREE)
 
-    def finish():
-        wait_sent(coarse_edge, last)
-        wait_sent(cons_edge, last + 1, LOW_SIDES)
-        for phase in range(DEGREE + 1):
-            wait_sent(field_edge(phase), phase)
-
-    return finish
-
-
-def stresses(sizes, field, cons, disp_out, rec_out, ind_out):
+    wait_sent(coarse_edge, last)
+    wait_sent(cons_edge, last + 1, LOW_SIDES)
+    for phase in range(DEGREE + 1):
+        wait_sent(field_edge(phase), phase)
+
+
+def stresses(sizes, field, cons, disp_out, rec_out, ind_out, rec, ind, out_sem):
     nx, ny, depth, kx, ky, slabs, planes = sizes
     first_x = lax.axis_index("slab") * nx
     first_y = lax.axis_index("plane") * ny
@@ -258,8 +257,16 @@
 
     scale_y = half((node_y >= 1) & (node_y <= total_y - 2)) * half((lane >= 1) & (lane <= depth - 2))
 
-    for c in range(3):
-        disp_out[c] = field[c, 1:nx + 1, OFF:OFF + ny, :]
+    inner = field.at[:, pl.ds(1, nx), pl.ds(OFF, ny)]
+    whole = pltpu.make_async_copy(inner, disp_out, out_sem.at[0])
+    whole.start()
+
+    def part(n):
+        here = pl.ds(n * ROWS_OUT, ROWS_OUT)
+        return (
+            pltpu.make_async_copy(rec.at[:, here], rec_out.at[:, here], out_sem.at[1 + 2 * n]),
+            pltpu.make_async_copy(ind.at[here], ind_out.at[here], out_sem.at[2 + 2 * n]),
+        )
 
     def corner_sums(c, i):
         low = field[c, i, pl.ds(OFF - 1, tall), :]
@@ -309,57 +316,72 @@
         inside = ((node_x >= 1) & (node_x <= total_x - 2)).astype(jnp.float32)
         scale = scale_y * (1.0 - 0.5 * inside)
         total = [(a + b) * scale for a, b in zip(before, after)]
-        rec = total[:6]
         for n in range(6):
-            rec_out[n, i - 1] = rec[n]
-        ind_out[i - 1] = total[6] - (
-            rec[0] * rec[0] + rec[1] * rec[1] + rec[2] * rec[2]
-            + 2.0 * (rec[3] * rec[3] + rec[4] * rec[4] + rec[5] * rec[5])
+            rec[n, i - 1] = total[n]
+        ind[i - 1] = total[6] - (
+            total[0] * total[0] + total[1] * total[1] + total[2] * total[2]
+            + 2.0 * (total[3] * total[3] + total[4] * total[4] + total[5] * total[5])
         )
         return after
 
-    lax.fori_loop(1, nx + 1, row, element_row(0))
-
-
-def whole_kernel(sizes, *refs):
-    inputs, outs, scratch = refs[:6], refs[6:9], refs[9:]
-    finish = smooth(sizes, inputs + scratch)
-    fields, cons = scratch[6], scratch[5]
-    stresses(sizes, fields.at[DEGREE], cons, *outs)
-    finish()
+    carry = element_row(0)
+    for n in range(nx // ROWS_OUT):
+        carry = lax.fori_loop(1 + n * ROWS_OUT, 1 + (n + 1) * ROWS_OUT, row, carry)
+        for copy in part(n):
+            copy.start()
+    whole.wait()
+    for n in range(nx // ROWS_OUT):
+        for copy in part(n):
+            copy.wait()
 
 
 def body(sizes, *blocks):
     nx, ny, depth, kx, ky, slabs, planes = sizes
-    any_spec = pl.BlockSpec(memory_space=pl.ANY)
-    vmem_spec = pl.BlockSpec(memory_space=pltpu.VMEM)
+    hbm = pl.BlockSpec(memory_space=pltpu.HBM)
+    vmem = pl.BlockSpec(memory_space=pltpu.VMEM)
     f32 = jnp.float32
-    return pl.pallas_call(
-        functools.partial(whole_kernel, sizes),
-        out_shape=(
-            jax.ShapeDtypeStruct((3, nx, ny, depth), f32),
-            jax.ShapeDtypeStruct((6, nx, ny, depth), f32),
-            jax.ShapeDtypeStruct((nx, ny, depth), f32),
-        ),
-        in_specs=[any_spec] * 6,
-        out_specs=(vmem_spec,) * 3,
+    padded = (
+        jax.ShapeDtypeStruct((3, nx + 2, ny + 16, depth), f32),
+        jax.ShapeDtypeStruct((nx + 1, ny + 16, depth), f32),
+    )
+    field, cons = pl.pallas_call(
+        functools.partial(smooth, sizes),
+        out_shape=padded,
+        in_specs=[hbm] * 6,
+        out_specs=(vmem,) * 2,
         scratch_shapes=[
             pltpu.VMEM((3, nx, ny, depth), f32),
             pltpu.VMEM((3, nx, ny, depth), f32),
             pltpu.VMEM((nx, ny, depth), f32),
             pltpu.VMEM((3, kx + 2, ky + 8, depth), f32),
             pltpu.VMEM((nx, ny), jnp.int32),
-            pltpu.VMEM((nx + 1, ny + 16, depth), f32),
-            pltpu.VMEM((DEGREE + 1, 3, nx + 2, ny + 16, depth), f32),
+            pltpu.VMEM((DEGREE, 3, nx + 2, ny + 16, depth), f32),
             pltpu.VMEM((3, nx, ny, depth), f32),
             pltpu.SemaphoreType.DMA((6,)),
             pltpu.SemaphoreType.DMA((DEGREE + 3, len(SIDES))),
             pltpu.SemaphoreType.DMA((DEGREE + 3, len(SIDES))),
         ],
         compiler_params=pltpu.CompilerParams(
-            collective_id=0, has_side_effects=True, vmem_limit_bytes=32 * 1024 * 1024
+            collective_id=0, has_side_effects=True, vmem_limit_bytes=VMEM_BYTES
         ),
     )(*blocks)
+    outs = (
+        jax.ShapeDtypeStruct((3, nx, ny, depth), f32),
+        jax.ShapeDtypeStruct((6, nx, ny, depth), f32),
+        jax.ShapeDtypeStruct((nx, ny, depth), f32),
+    )
+    return pl.pallas_call(
+        functools.partial(stresses, sizes),
+        out_shape=outs,
+        in_specs=[vmem] * 2,
+        out_specs=(hbm,) * 3,
+        scratch_shapes=[
+            pltpu.VMEM(outs[1].shape, f32),
+            pltpu.VMEM(outs[2].shape, f32),
+            pltpu.SemaphoreType.DMA((1 + 2 * (nx // ROWS_OUT),)),
+        ],
+        compiler_params=pltpu.CompilerParams(vmem_limit_bytes=VMEM_BYTES),
+    )(field, cons)
 
 
 def solution(mesh):

time: 44.6 us -> 39.4 us (0.88)
  local copies, waits for them, and re-layouts: 7.66 us -> 0 us
  Pallas kernels: 36 us -> 38.6 us
    unnamed x15 -> x0, local copies, waits for them, and re-layouts: 7.66 us -> none
    pallas_call x1 -> x2, Pallas kernels: 36 us -> 38.6 us  [the longest x1 32.9 us: body(): pl.pallas_call(functools.partial(smooth, sizes), out_shape=padded, in_spe...]
where the time goes in v2:
time: 39.4 us; the launch traced here: 39.3 us
  Pallas kernels  38.6 us (98%)
  between operations  0.64 us (2%)
    pallas_call x1, Pallas kernels, body(): pl.pallas_call(functools.partial(smooth, sizes), out_shape=padded, in_spe...  32.9 us
    pallas_call x1, Pallas kernels, body(): pl.pallas_call(functools.partial(stresses, sizes), out_shape=outs, in_spe...  5.74 us

profile of v2, /device:TPU:0, one launch (start us, length us, event | category | flops | bytes accessed | tf_op | source)
XLA Modules:
  0.0 39.3 jit_solution(15166184831538437382)
XLA Ops:
  0.6 32.9 %shard_map.85 = (f32[3,18,32,128]{3,2,1,0:T(8,128)}, f32[17,32,128]{2,1,0:T(8,128)}) custom-call(f32[3,16,16,128]{3,2,1,0:T(8,128)} %refs_0_.1, f32[3,16,16,128]{3,2,1,0:T(8,128)} %refs_1_.1, f32[16,16,128]{2,1,0:T(8,128)} %refs_2_.1, f32[3,8,8,128]{3,2,1,0:T(8,128)} %refs_3_.1, s32[16,16]{1,0:T(8,128)} %refs_4_.1, f32[16,16,128]{2,1,0:T(8,128)} %refs_5_.1), custom_call_target="tpu_custom_call" | custom-call | tf_op jit(solution)/shard_map/pallas_call | solution.py:347
  33.5 5.7 %shard_map.86 = (f32[3,16,16,128]{3,2,1,0:T(8,128)}, f32[6,16,16,128]{3,2,1,0:T(8,128)}, f32[16,16,128]{2,1,0:T(8,128)}) custom-call(f32[3,18,32,128]{3,2,1,0:T(8,128)} %get-tuple-element.5.field, f32[17,32,128]{2,1,0:T(8,128)} %get-tuple-element.6.cons), custom_call_target="tpu_custom_call" | custom-call | tf_op jit(solution)/shard_map/pallas_call | solution.py:373

commit v3 on v2

--- a/solution.py
+++ b/solution.py
@@ -190,7 +190,7 @@
     loads[4].wait()
     loads[5].wait()
 
-    rows = 4
+    rows = nx
     rho = 1.0 / SIGMA
     for phase in range(DEGREE):
         wait_arrived(field_edge(phase), phase)
@@ -326,7 +326,7 @@
 
     carry = element_row(0)
     for n in range(nx // ROWS_OUT):
-        carry = lax.fori_loop(1 + n * ROWS_OUT, 1 + (n + 1) * ROWS_OUT, row, carry)
+        carry = lax.fori_loop(1 + n * ROWS_OUT, 1 + (n + 1) * ROWS_OUT, row, carry, unroll=True)
         for copy in part(n):
             copy.start()
     whole.wait()

time: 39.4 us -> 34.7 us (0.88)
  Pallas kernels: 38.6 us -> 33.9 us
    pallas_call x1, Pallas kernels: 32.9 us -> 29.7 us  [body(): pl.pallas_call(functools.partial(smooth, sizes), out_shape=padded, in_spe...]
    pallas_call x1, Pallas kernels: 5.74 us -> 4.12 us  [body(): pl.pallas_call(functools.partial(stresses, sizes), out_shape=outs, in_spe...]
where the time goes in v3:
time: 34.7 us; the launch traced here: 34.5 us
  Pallas kernels  33.9 us (98%)
  between operations  0.64 us (2%)
    pallas_call x1, Pallas kernels, body(): pl.pallas_call(functools.partial(smooth, sizes), out_shape=padded, in_spe...  29.7 us
    pallas_call x1, Pallas kernels, body(): pl.pallas_call(functools.partial(stresses, sizes), out_shape=outs, in_spe...  4.12 us

profile of v3, /device:TPU:0, one launch (start us, length us, event | category | flops | bytes accessed | tf_op | source)
XLA Modules:
  0.0 34.5 jit_solution(14556657470904992338)
XLA Ops:
  0.6 29.7 %shard_map.85 = (f32[3,18,32,128]{3,2,1,0:T(8,128)}, f32[17,32,128]{2,1,0:T(8,128)}) custom-call(f32[3,16,16,128]{3,2,1,0:T(8,128)} %refs_0_.1, f32[3,16,16,128]{3,2,1,0:T(8,128)} %refs_1_.1, f32[16,16,128]{2,1,0:T(8,128)} %refs_2_.1, f32[3,8,8,128]{3,2,1,0:T(8,128)} %refs_3_.1, s32[16,16]{1,0:T(8,128)} %refs_4_.1, f32[16,16,128]{2,1,0:T(8,128)} %refs_5_.1), custom_call_target="tpu_custom_call" | custom-call | tf_op jit(solution)/shard_map/pallas_call | solution.py:347
  30.4 4.1 %shard_map.86 = (f32[3,16,16,128]{3,2,1,0:T(8,128)}, f32[6,16,16,128]{3,2,1,0:T(8,128)}, f32[16,16,128]{2,1,0:T(8,128)}) custom-call(f32[3,18,32,128]{3,2,1,0:T(8,128)} %get-tuple-element.5.field, f32[17,32,128]{2,1,0:T(8,128)} %get-tuple-element.6.cons), custom_call_target="tpu_custom_call" | custom-call | tf_op jit(solution)/shard_map/pallas_call | solution.py:373

commit v4 on v3

--- a/solution.py
+++ b/solution.py
@@ -46,7 +46,8 @@
 def smooth(sizes, *refs):
     nx, ny, depth, kx, ky, slabs, planes = sizes
     (start_hbm, load_hbm, shift_hbm, coarse_hbm, agg_hbm, cons_hbm, final, cons,
-     start, load, shift, table, agg, earlier, resid, in_sem, send_sem, recv_sem) = refs
+     start, load, shift, table, agg, earlier, resid, halo_x, halo_y, border_y,
+     in_sem, send_sem, recv_sem) = refs
     fields = [earlier.at[n] for n in range(DEGREE)] + [final]
     slab = lax.axis_index("slab")
     plane = lax.axis_index("plane")
@@ -72,6 +73,12 @@
     table[:, 0, 0:ky, :] = zero_table
     table[:, kx + 1, 0:ky, :] = zero_table
 
+    zero_side = jnp.zeros((3, ny + 16, depth), jnp.float32)
+    for phase in range(DEGREE):
+        for side in range(2):
+            halo_x[phase, side] = zero_side
+            halo_y[phase, side] = jnp.zeros((3, nx + 16, depth), jnp.float32)
+
     barrier = pltpu.get_barrier_semaphore()
     for step_x, step_y in SIDES:
         @pl.when(exists(step_x, step_y))
@@ -80,20 +87,12 @@
                 barrier, inc=1, device_id=(slab + step_x, plane + step_y), device_id_type=MESH
             )
 
-    zero_row = jnp.zeros((nx + 2, depth), jnp.float32)
-    for step_x, step_y in ((0, 1), (0, -1), (1, 0), (-1, 0)):
-        @pl.when(jnp.logical_not(exists(-step_x, -step_y)))
-        def _():
-            for phase in range(DEGREE + 1):
-                for c in range(3):
-                    if step_y:
-                        row = OFF - 1 if step_y > 0 else OFF + ny
-                        for i in range(nx + 2):
-                            fields[phase][c, i, row:row + 1, :] = zero_row[0:1]
-                    else:
-                        i = 0 if step_x > 0 else nx + 1
-                        for at in range(0, ny + 16, 8):
-                            fields[phase][c, i, at:at + 8, :] = zero_row[0:8]
+    for field in fields[:DEGREE]:
+        field[:, 0] = zero_side
+        field[:, nx + 1] = zero_side
+        for i in range(1, nx + 1):
+            field[:, i, 0:OFF, :] = zero_side[:, 0:OFF]
+            field[:, i, OFF + ny:OFF + ny + 8, :] = zero_side[:, 0:8]
 
     near_x = 1 + (slab > 0).astype(jnp.int32) + (slab < slabs - 1).astype(jnp.int32)
     near_y = 1 + (plane > 0).astype(jnp.int32) + (plane < planes - 1).astype(jnp.int32)
@@ -144,12 +143,39 @@
             cons.at[to_x, to_y],
         )
 
-    def field_edge(phase):
+    def field_edge(step_x, step_y):
+        from_x, to_x = edge(step_x, 1, nx)
+        from_y, to_y = edge(step_y, OFF, ny)
+        return final.at[:, from_x, from_y], final.at[:, to_x, to_y]
+
+    def halo_edge(phase):
         def make(step_x, step_y):
-            from_x, to_x = edge(step_x, 1, nx)
-            from_y, to_y = edge(step_y, OFF, ny)
-            return fields[phase].at[:, from_x, from_y], fields[phase].at[:, to_x, to_y]
+            row = nx if step_x > 0 else 1
+            to_x, to_y = int(step_x < 0), int(step_y < 0)
+            if step_y == 0:
+                return (
+                    fields[phase].at[:, row, pl.ds(OFF, ny)],
+                    halo_x.at[phase, to_x, :, pl.ds(OFF, ny)],
+                )
+            border = border_y.at[phase, 1 - to_y]
+            if step_x == 0:
+                return border, halo_y.at[phase, to_y, :, pl.ds(OFF, nx)]
+            corner = OFF - 1 if step_y > 0 else OFF + ny
+            return border.at[:, pl.ds(row - 1, 1)], halo_x.at[phase, to_x, :, pl.ds(corner, 1)]
         return make
+
+    def column(ref, side, tall, first):
+        lines = ref.reshape(ref.shape[0] * tall, depth)
+        return lines, pl.ds(first + side * (ny - 1), nx, stride=tall)
+
+    def field_column(phase, c, side):
+        return column(fields[phase].at[c], side, ny + 16, ny + 16 + OFF)
+
+    def fill_border(phase):
+        for c in range(3):
+            for side in range(2):
+                lines, where = field_column(phase, c, side)
+                border_y[phase, side, c] = lines[where, :]
 
     last = DEGREE + 1
     start_all(coarse_edge, last)
@@ -169,8 +195,8 @@
     slots = lax.broadcasted_iota(jnp.int32, (ny, deep), 1).astype(jnp.float32)
     picks = []
     for i in range(nx):
-        column = jnp.sum(jnp.where(own, place[i:i + 1, :], 0.0), axis=1, keepdims=True)
-        picks.append((column == slots).astype(jnp.bfloat16))
+        target = jnp.sum(jnp.where(own, place[i:i + 1, :], 0.0), axis=1, keepdims=True)
+        picks.append((target == slots).astype(jnp.bfloat16))
     pick = jnp.concatenate(picks, axis=0)
     loads[0].wait()
     loads[2].wait()
@@ -185,59 +211,86 @@
             moved = piece if moved is None else moved + piece
         fields[0][c, 1:nx + 1, OFF:OFF + ny, :] = start[c] + moved.reshape(nx, ny, depth)
 
-    start_all(field_edge(0), 0)
+    fill_border(0)
+    start_all(halo_edge(0), 0)
     start_all(cons_edge, last + 1, LOW_SIDES)
     loads[4].wait()
     loads[5].wait()
 
-    rows = nx
     rho = 1.0 / SIGMA
+    keep, gain = None, 1.0 / THETA
     for phase in range(DEGREE):
-        wait_arrived(field_edge(phase), phase)
         if phase:
             rho_new = 1.0 / (2.0 * SIGMA - rho)
             keep, gain = rho_new * rho, 2.0 * rho_new / DELTA_C
             rho = rho_new
 
-        def chunk(at, carry):
-            c = at // (nx // rows)
-            first = (at % (nx // rows)) * rows
-            span = pl.ds(first, rows + 2)
+        def own_block(c, carry):
             along_y = (
-                fields[phase][c, span, pl.ds(OFF - 1, ny), :]
-                + fields[phase][c, span, pl.ds(OFF, ny), :]
-                + fields[phase][c, span, pl.ds(OFF + 1, ny), :]
+                fields[phase][c, :, pl.ds(OFF - 1, ny), :]
+                + fields[phase][c, :, pl.ds(OFF, ny), :]
+                + fields[phase][c, :, pl.ds(OFF + 1, ny), :]
             )
             boxed = box_z(along_y[:-2] + along_y[1:-1] + along_y[2:])
-            centre = fields[phase][c, pl.ds(first + 1, rows), pl.ds(OFF, ny), :]
-            here = pl.ds(first, rows)
-            applied = (3.0 + shift[here]) * centre - boxed * (1.0 / 3.0)
+            inner = (c, pl.ds(1, nx), pl.ds(OFF, ny))
+            centre = fields[phase][inner]
+            applied = (3.0 + shift[...]) * centre - boxed * (1.0 / 3.0)
             if phase == 0:
-                left = load[c, here] - applied
-                direction = left * (1.0 / THETA)
+                left = load[c] - applied
+                direction = left * gain
             else:
-                left = resid[c, here] - applied
+                left = resid[c] - applied
                 direction = keep * centre + gain * left
-            inner = (c, pl.ds(first + 1, rows), pl.ds(OFF, ny))
             if phase < DEGREE - 1:
-                resid[c, here] = left
+                resid[c] = left
             else:
                 for n in range(DEGREE):
                     direction = direction + fields[n][inner]
             fields[phase + 1][inner] = direction
             return carry
 
-        lax.fori_loop(0, 3 * (nx // rows), chunk, 0)
-        start_all(field_edge(phase + 1), phase + 1)
+        lax.fori_loop(0, 3, own_block, 0)
+
+        wait_arrived(halo_edge(phase), phase)
+        from_y, from_x = {}, {}
+        for c in range(3):
+            for side in range(2):
+                for halo, given, count in ((halo_y, from_y, nx), (halo_x, from_x, ny)):
+                    line = (
+                        halo[phase, side, c, pl.ds(OFF - 1, count), :]
+                        + halo[phase, side, c, pl.ds(OFF, count), :]
+                        + halo[phase, side, c, pl.ds(OFF + 1, count), :]
+                    )
+                    given[c, side] = box_z(line) * (1.0 / 3.0)
+        for c in range(3):
+            for side in range(2):
+                lines, where = field_column(phase + 1, c, side)
+                lines[where, :] = lines[where, :] + gain * from_y[c, side]
+            for side in range(2):
+                at = (c, 1 + side * (nx - 1), pl.ds(OFF, ny))
+                fields[phase + 1][at] = fields[phase + 1][at] + gain * from_x[c, side]
+        if phase < DEGREE - 1:
+            fill_border(phase + 1)
+            start_all(halo_edge(phase + 1), phase + 1)
+            for c in range(3):
+                for side in range(2):
+                    lines, where = column(resid.at[c], side, ny, 0)
+                    lines[where, :] = lines[where, :] + from_y[c, side]
+                for side in range(2):
+                    at = (c, side * (nx - 1))
+                    resid[at] = resid[at] + from_x[c, side]
+        else:
+            start_all(field_edge, DEGREE)
 
     loads[3].wait()
     wait_arrived(cons_edge, last + 1, LOW_SIDES)
-    wait_arrived(field_edge(DEGREE), DEGREE)
+    wait_arrived(field_edge, DEGREE)
 
     wait_sent(coarse_edge, last)
     wait_sent(cons_edge, last + 1, LOW_SIDES)
-    for phase in range(DEGREE + 1):
-        wait_sent(field_edge(phase), phase)
+    for phase in range(DEGREE):
+        wait_sent(halo_edge(phase), phase)
+    wait_sent(field_edge, DEGREE)
 
 
 def stresses(sizes, field, cons, disp_out, rec_out, ind_out, rec, ind, out_sem):
@@ -357,6 +410,9 @@
             pltpu.VMEM((nx, ny), jnp.int32),
             pltpu.VMEM((DEGREE, 3, nx + 2, ny + 16, depth), f32),
             pltpu.VMEM((3, nx, ny, depth), f32),
+            pltpu.VMEM((DEGREE, 2, 3, ny + 16, depth), f32),
+            pltpu.VMEM((DEGREE, 2, 3, nx + 16, depth), f32),
+            pltpu.VMEM((DEGREE, 2, 3, nx, depth), f32),
             pltpu.SemaphoreType.DMA((6,)),
             pltpu.SemaphoreType.DMA((DEGREE + 3, len(SIDES))),
             pltpu.SemaphoreType.DMA((DEGREE + 3, len(SIDES))),

time: 34.7 us -> 33.4 us (0.963)
  Pallas kernels: 33.9 us -> 32.6 us
    pallas_call x1, Pallas kernels: 29.7 us -> 28.5 us  [body(): pl.pallas_call(functools.partial(smooth, sizes), out_shape=padded, in_spe...]
where the time goes in v4:
time: 33.4 us; the launch traced here: 33.3 us
  Pallas kernels  32.6 us (98%)
  between operations  0.64 us (2%)
    pallas_call x1, Pallas kernels, body(): pl.pallas_call(functools.partial(smooth, sizes), out_shape=padded, in_spe...  28.5 us
    pallas_call x1, Pallas kernels, body(): pl.pallas_call(functools.partial(stresses, sizes), out_shape=outs, in_spe...  4.12 us

profile of v4, /device:TPU:0, one launch (start us, length us, event | category | flops | bytes accessed | tf_op | source)
XLA Modules:
  0.0 33.3 jit_solution(7033619113724296410)
XLA Ops:
  0.6 28.5 %shard_map.85 = (f32[3,18,32,128]{3,2,1,0:T(8,128)}, f32[17,32,128]{2,1,0:T(8,128)}) custom-call(f32[3,16,16,128]{3,2,1,0:T(8,128)} %refs_0_.1, f32[3,16,16,128]{3,2,1,0:T(8,128)} %refs_1_.1, f32[16,16,128]{2,1,0:T(8,128)} %refs_2_.1, f32[3,8,8,128]{3,2,1,0:T(8,128)} %refs_3_.1, s32[16,16]{1,0:T(8,128)} %refs_4_.1, f32[16,16,128]{2,1,0:T(8,128)} %refs_5_.1), custom_call_target="tpu_custom_call" | custom-call | tf_op jit(solution)/shard_map/pallas_call | solution.py:400
  29.2 4.1 %shard_map.86 = (f32[3,16,16,128]{3,2,1,0:T(8,128)}, f32[6,16,16,128]{3,2,1,0:T(8,128)}, f32[16,16,128]{2,1,0:T(8,128)}) custom-call(f32[3,18,32,128]{3,2,1,0:T(8,128)} %get-tuple-element.5.field, f32[17,32,128]{2,1,0:T(8,128)} %get-tuple-element.6.cons), custom_call_target="tpu_custom_call" | custom-call | tf_op jit(solution)/shard_map/pallas_call | solution.py:429

commit v5 on v3

--- a/solution.py
+++ b/solution.py
@@ -19,11 +19,11 @@
 LOW_SIDES = ((0, 1), (1, 1), (1, 0))
 
 
-def edge(step, first, count):
+def edge(step, first, count, width=1):
     if step > 0:
-        return pl.ds(first + count - 1, 1), pl.ds(first - 1, 1)
+        return pl.ds(first + count - width, width), pl.ds(first - width, width)
     if step < 0:
-        return pl.ds(first, 1), pl.ds(first + count, 1)
+        return pl.ds(first, width), pl.ds(first + count, width)
     return pl.ds(first, count), pl.ds(first, count)
 
 
@@ -46,8 +46,8 @@
 def smooth(sizes, *refs):
     nx, ny, depth, kx, ky, slabs, planes = sizes
     (start_hbm, load_hbm, shift_hbm, coarse_hbm, agg_hbm, cons_hbm, final, cons,
-     start, load, shift, table, agg, earlier, resid, in_sem, send_sem, recv_sem) = refs
-    fields = [earlier.at[n] for n in range(DEGREE)] + [final]
+     start, load, shift, table, agg, earlier, resid, resid_sent, in_sem, send_sem, recv_sem) = refs
+    fields = [earlier.at[n] for n in range(DEGREE)]
     slab = lax.axis_index("slab")
     plane = lax.axis_index("plane")
 
@@ -60,8 +60,10 @@
         pltpu.make_async_copy(agg_hbm, agg, in_sem.at[1]),
         pltpu.make_async_copy(start_hbm, start, in_sem.at[2]),
         pltpu.make_async_copy(cons_hbm, cons.at[pl.ds(1, nx), pl.ds(OFF, ny)], in_sem.at[3]),
-        pltpu.make_async_copy(load_hbm, load, in_sem.at[4]),
-        pltpu.make_async_copy(shift_hbm, shift, in_sem.at[5]),
+        pltpu.make_async_copy(
+            load_hbm, load.at[:, pl.ds(1, nx), pl.ds(OFF, ny)], in_sem.at[4]
+        ),
+        pltpu.make_async_copy(shift_hbm, shift.at[pl.ds(1, nx), pl.ds(OFF, ny)], in_sem.at[5]),
     ]
     for copy in loads:
         copy.start()
@@ -71,6 +73,14 @@
         table[:, a, ky:ky + 8, :] = zero_table
     table[:, 0, 0:ky, :] = zero_table
     table[:, kx + 1, 0:ky, :] = zero_table
+
+    for field in (fields[0], fields[2]):
+        for i in range(nx + 4):
+            if i < 2 or i >= nx + 2:
+                field[:, i] = jnp.zeros((3, ny + 16, depth), jnp.float32)
+            else:
+                field[:, i, 0:OFF, :] = zero_table
+                field[:, i, OFF + ny:OFF + ny + 8, :] = zero_table
 
     barrier = pltpu.get_barrier_semaphore()
     for step_x, step_y in SIDES:
@@ -80,21 +90,6 @@
                 barrier, inc=1, device_id=(slab + step_x, plane + step_y), device_id_type=MESH
             )
 
-    zero_row = jnp.zeros((nx + 2, depth), jnp.float32)
-    for step_x, step_y in ((0, 1), (0, -1), (1, 0), (-1, 0)):
-        @pl.when(jnp.logical_not(exists(-step_x, -step_y)))
-        def _():
-            for phase in range(DEGREE + 1):
-                for c in range(3):
-                    if step_y:
-                        row = OFF - 1 if step_y > 0 else OFF + ny
-                        for i in range(nx + 2):
-                            fields[phase][c, i, row:row + 1, :] = zero_row[0:1]
-                    else:
-                        i = 0 if step_x > 0 else nx + 1
-                        for at in range(0, ny + 16, 8):
-                            fields[phase][c, i, at:at + 8, :] = zero_row[0:8]
-
     near_x = 1 + (slab > 0).astype(jnp.int32) + (slab < slabs - 1).astype(jnp.int32)
     near_y = 1 + (plane > 0).astype(jnp.int32) + (plane < planes - 1).astype(jnp.int32)
     pl.semaphore_wait(barrier, near_x * near_y - 1)
@@ -136,23 +131,36 @@
             to_y = pl.ds(ky + 7, 1)
         return coarse_hbm.at[:, from_x, from_y], table.at[:, to_x, to_y]
 
-    def cons_edge(step_x, step_y):
-        from_x, to_x = edge(step_x, 1, nx)
-        from_y, to_y = edge(step_y, OFF, ny)
-        return (
-            cons_hbm.at[pl.ds(from_x.start - 1, from_x.size), pl.ds(from_y.start - OFF, from_y.size)],
-            cons.at[to_x, to_y],
-        )
-
-    def field_edge(phase):
+    def input_edge(source, target):
+        lead = (slice(None),) * (len(source.shape) - 3)
+
         def make(step_x, step_y):
             from_x, to_x = edge(step_x, 1, nx)
             from_y, to_y = edge(step_y, OFF, ny)
-            return fields[phase].at[:, from_x, from_y], fields[phase].at[:, to_x, to_y]
+            from_x = pl.ds(from_x.start - 1, from_x.size)
+            from_y = pl.ds(from_y.start - OFF, from_y.size)
+            return source.at[lead + (from_x, from_y)], target.at[lead + (to_x, to_y)]
         return make
 
-    last = DEGREE + 1
-    start_all(coarse_edge, last)
+    def field_edge(field, width):
+        def make(step_x, step_y):
+            from_x, to_x = edge(step_x, width, nx, width)
+            from_y, to_y = edge(step_y, OFF, ny, width)
+            return field.at[:, from_x, from_y], field.at[:, to_x, to_y]
+        return make
+
+    coarse_go = (coarse_edge, 0)
+    load_go = (input_edge(load_hbm, load), 1)
+    shift_go = (input_edge(shift_hbm, shift), 2)
+    cons_go = (input_edge(cons_hbm, cons), 3, LOW_SIDES)
+    first_go = (field_edge(fields[0], 2), 4)
+    middle_go = (field_edge(fields[2], 2), 5)
+    resid_go = (field_edge(resid_sent, 1), 6)
+    final_go = (field_edge(final, 1), 7)
+    start_all(*coarse_go)
+    start_all(*load_go)
+    start_all(*shift_go)
+    start_all(*cons_go)
 
     loads[1].wait()
     cols = ky * planes
@@ -174,7 +182,7 @@
     pick = jnp.concatenate(picks, axis=0)
     loads[0].wait()
     loads[2].wait()
-    wait_arrived(coarse_edge, last)
+    wait_arrived(*coarse_go)
     for c in range(3):
         rest = table[c].reshape(deep, depth)
         moved = None
@@ -183,61 +191,91 @@
             rest = rest - part.astype(jnp.float32)
             piece = jnp.dot(pick, part, preferred_element_type=jnp.float32)
             moved = piece if moved is None else moved + piece
-        fields[0][c, 1:nx + 1, OFF:OFF + ny, :] = start[c] + moved.reshape(nx, ny, depth)
-
-    start_all(field_edge(0), 0)
-    start_all(cons_edge, last + 1, LOW_SIDES)
+        fields[0][c, 2:nx + 2, OFF:OFF + ny, :] = start[c] + moved.reshape(nx, ny, depth)
+
+    start_all(*first_go)
     loads[4].wait()
     loads[5].wait()
-
-    rows = nx
+    wait_arrived(*load_go)
+    wait_arrived(*shift_go)
+    wait_arrived(*first_go)
+
+    rows = nx // 2 + 1
+    first_x, first_y = slab * nx, plane * ny
+    lines = lax.broadcasted_iota(jnp.int32, (rows, ny + 8, depth), 1) + (first_y - 1)
+    across = lax.broadcasted_iota(jnp.int32, (rows, ny + 8, depth), 0) + (first_x - 1)
+    in_mesh_y = (lines >= 0) & (lines < ny * planes)
+
+    def stencil(phase, c, first, count, top, tall):
+        field = fields[phase]
+        span = pl.ds(first - 1, count + 2)
+        along_y = (
+            field[c, span, pl.ds(top - 1, tall), :]
+            + field[c, span, pl.ds(top, tall), :]
+            + field[c, span, pl.ds(top + 1, tall), :]
+        )
+        boxed = box_z(along_y[:-2] + along_y[1:-1] + along_y[2:])
+        centre = field[c, pl.ds(first, count), pl.ds(top, tall), :]
+        here = shift[pl.ds(first - 1, count), pl.ds(top, tall), :]
+        return centre, (3.0 + here) * centre - boxed * (1.0 / 3.0)
+
     rho = 1.0 / SIGMA
+    keep, gain = 0.0, 1.0 / THETA
     for phase in range(DEGREE):
-        wait_arrived(field_edge(phase), phase)
         if phase:
             rho_new = 1.0 / (2.0 * SIGMA - rho)
             keep, gain = rho_new * rho, 2.0 * rho_new / DELTA_C
             rho = rho_new
-
-        def chunk(at, carry):
-            c = at // (nx // rows)
-            first = (at % (nx // rows)) * rows
-            span = pl.ds(first, rows + 2)
-            along_y = (
-                fields[phase][c, span, pl.ds(OFF - 1, ny), :]
-                + fields[phase][c, span, pl.ds(OFF, ny), :]
-                + fields[phase][c, span, pl.ds(OFF + 1, ny), :]
+        if phase == 2:
+            wait_arrived(*middle_go)
+            wait_arrived(*resid_go)
+
+        def wide(at, carry):
+            c = at // 2
+            first = 1 + (at % 2) * rows
+            centre, applied = stencil(phase, c, first, rows, OFF - 1, ny + 8)
+            where = (c, pl.ds(first - 1, rows), pl.ds(OFF - 1, ny + 8))
+            left = (load if phase == 0 else resid_sent)[where] - applied
+            direction = gain * left
+            if phase:
+                direction = direction + keep * centre
+            node_x = across + (first - 1)
+            inside = in_mesh_y & (node_x >= 0) & (node_x < nx * slabs)
+            resid[where] = left
+            fields[phase + 1][c, pl.ds(first, rows), pl.ds(OFF - 1, ny + 8), :] = jnp.where(
+                inside, direction, 0.0
             )
-            boxed = box_z(along_y[:-2] + along_y[1:-1] + along_y[2:])
-            centre = fields[phase][c, pl.ds(first + 1, rows), pl.ds(OFF, ny), :]
-            here = pl.ds(first, rows)
-            applied = (3.0 + shift[here]) * centre - boxed * (1.0 / 3.0)
-            if phase == 0:
-                left = load[c, here] - applied
-                direction = left * (1.0 / THETA)
-            else:
-                left = resid[c, here] - applied
-                direction = keep * centre + gain * left
-            inner = (c, pl.ds(first + 1, rows), pl.ds(OFF, ny))
+            return carry
+
+        def narrow(c, carry):
+            centre, applied = stencil(phase, c, 2, nx, OFF, ny)
+            where = (c, pl.ds(1, nx), pl.ds(OFF, ny))
+            inner = (c, pl.ds(2, nx), pl.ds(OFF, ny))
+            left = resid[where] - applied
+            direction = keep * centre + gain * left
             if phase < DEGREE - 1:
-                resid[c, here] = left
+                resid_sent[where] = left
+                fields[phase + 1][inner] = direction
             else:
                 for n in range(DEGREE):
                     direction = direction + fields[n][inner]
-            fields[phase + 1][inner] = direction
+                final[where] = direction
             return carry
 
-        lax.fori_loop(0, 3 * (nx // rows), chunk, 0)
-        start_all(field_edge(phase + 1), phase + 1)
+        if phase % 2 == 0:
+            lax.fori_loop(0, 6, wide, 0)
+        else:
+            lax.fori_loop(0, 3, narrow, 0)
+        if phase == 1:
+            start_all(*middle_go)
+            start_all(*resid_go)
+    start_all(*final_go)
 
     loads[3].wait()
-    wait_arrived(cons_edge, last + 1, LOW_SIDES)
-    wait_arrived(field_edge(DEGREE), DEGREE)
-
-    wait_sent(coarse_edge, last)
-    wait_sent(cons_edge, last + 1, LOW_SIDES)
-    for phase in range(DEGREE + 1):
-        wait_sent(field_edge(phase), phase)
+    wait_arrived(*cons_go)
+    wait_arrived(*final_go)
+    for go in (coarse_go, load_go, shift_go, cons_go, first_go, middle_go, resid_go, final_go):
+        wait_sent(*go)
 
 
 def stresses(sizes, field, cons, disp_out, rec_out, ind_out, rec, ind, out_sem):
@@ -351,15 +389,16 @@
         out_specs=(vmem,) * 2,
         scratch_shapes=[
             pltpu.VMEM((3, nx, ny, depth), f32),
-            pltpu.VMEM((3, nx, ny, depth), f32),
-            pltpu.VMEM((nx, ny, depth), f32),
+            pltpu.VMEM((3, nx + 2, ny + 16, depth), f32),
+            pltpu.VMEM((nx + 2, ny + 16, depth), f32),
             pltpu.VMEM((3, kx + 2, ky + 8, depth), f32),
             pltpu.VMEM((nx, ny), jnp.int32),
-            pltpu.VMEM((DEGREE, 3, nx + 2, ny + 16, depth), f32),
-            pltpu.VMEM((3, nx, ny, depth), f32),
+            pltpu.VMEM((DEGREE, 3, nx + 4, ny + 16, depth), f32),
+            pltpu.VMEM((3, nx + 2, ny + 16, depth), f32),
+            pltpu.VMEM((3, nx + 2, ny + 16, depth), f32),
             pltpu.SemaphoreType.DMA((6,)),
-            pltpu.SemaphoreType.DMA((DEGREE + 3, len(SIDES))),
-            pltpu.SemaphoreType.DMA((DEGREE + 3, len(SIDES))),
+            pltpu.SemaphoreType.DMA((8, len(SIDES))),
+            pltpu.SemaphoreType.DMA((8, len(SIDES))),
         ],
         compiler_params=pltpu.CompilerParams(
             collective_id=0, has_side_effects=True, vmem_limit_bytes=VMEM_BYTES

time: 34.7 us -> 31.6 us (0.911)
  the two profiles are of different devices: /device:TPU:0 before, /device:TPU:3 now
where the time goes in v5:
time: 31.6 us; the launch traced here: 31.5 us
  Pallas kernels  30.8 us (97%)
  between operations  0.64 us (2%)
    pallas_call x1, Pallas kernels, body(): pl.pallas_call(functools.partial(smooth, sizes), out_shape=padded, in_spe...  26.7 us
    pallas_call x1, Pallas kernels, body(): pl.pallas_call(functools.partial(stresses, sizes), out_shape=outs, in_spe...  4.12 us

profile of v5, /device:TPU:3, one launch (start us, length us, event | category | flops | bytes accessed | tf_op | source)
XLA Modules:
  0.0 31.5 jit_solution(8766041591678150109)
XLA Ops:
  0.6 26.7 %shard_map.85 = (f32[3,18,32,128]{3,2,1,0:T(8,128)}, f32[17,32,128]{2,1,0:T(8,128)}) custom-call(f32[3,16,16,128]{3,2,1,0:T(8,128)} %refs_0_.1, f32[3,16,16,128]{3,2,1,0:T(8,128)} %refs_1_.1, f32[16,16,128]{2,1,0:T(8,128)} %refs_2_.1, f32[3,8,8,128]{3,2,1,0:T(8,128)} %refs_3_.1, s32[16,16]{1,0:T(8,128)} %refs_4_.1, f32[16,16,128]{2,1,0:T(8,128)} %refs_5_.1), custom_call_target="tpu_custom_call" | custom-call | tf_op jit(solution)/shard_map/pallas_call | solution.py:385
  27.4 4.1 %shard_map.86 = (f32[3,16,16,128]{3,2,1,0:T(8,128)}, f32[6,16,16,128]{3,2,1,0:T(8,128)}, f32[16,16,128]{2,1,0:T(8,128)}) custom-call(f32[3,18,32,128]{3,2,1,0:T(8,128)} %get-tuple-element.5.field, f32[17,32,128]{2,1,0:T(8,128)} %get-tuple-element.6.cons), custom_call_target="tpu_custom_call" | custom-call | tf_op jit(solution)/shard_map/pallas_call | solution.py:412

commit v6 on v5

--- a/solution.py
+++ b/solution.py
@@ -13,7 +13,7 @@
 SIGMA = THETA / DELTA_C
 MESH = pl.DeviceIdType.MESH
 OFF = 8
-SIDES = ((0, 1), (0, -1), (1, 1), (1, -1), (-1, 1), (-1, -1), (1, 0), (-1, 0))
+SIDES = ((1, 1), (1, -1), (-1, 1), (-1, -1), (0, 1), (0, -1), (1, 0), (-1, 0))
 VMEM_BYTES = 56 * 1024 * 1024
 ROWS_OUT = 4
 LOW_SIDES = ((0, 1), (1, 1), (1, 0))
@@ -273,9 +273,10 @@
 
     loads[3].wait()
     wait_arrived(*cons_go)
+    for go in (coarse_go, load_go, shift_go, cons_go, first_go, middle_go, resid_go):
+        wait_sent(*go)
     wait_arrived(*final_go)
-    for go in (coarse_go, load_go, shift_go, cons_go, first_go, middle_go, resid_go, final_go):
-        wait_sent(*go)
+    wait_sent(*final_go)
 
 
 def stresses(sizes, field, cons, disp_out, rec_out, ind_out, rec, ind, out_sem):

time: 31.6 us -> 30.1 us (0.953)
  the two profiles are of different devices: /device:TPU:3 before, /device:TPU:0 now
where the time goes in v6:
time: 30.1 us; the launch traced here: 30 us
  Pallas kernels  29.3 us (97%)
  between operations  0.64 us (2%)
    pallas_call x1, Pallas kernels, body(): pl.pallas_call(functools.partial(smooth, sizes), out_shape=padded, in_spe...  25.2 us
    pallas_call x1, Pallas kernels, body(): pl.pallas_call(functools.partial(stresses, sizes), out_shape=outs, in_spe...  4.12 us

profile of v6, /device:TPU:0, one launch (start us, length us, event | category | flops | bytes accessed | tf_op | source)
XLA Modules:
  0.0 30.0 jit_solution(4470224313991542590)
XLA Ops:
  0.6 25.2 %shard_map.85 = (f32[3,18,32,128]{3,2,1,0:T(8,128)}, f32[17,32,128]{2,1,0:T(8,128)}) custom-call(f32[3,16,16,128]{3,2,1,0:T(8,128)} %refs_0_.1, f32[3,16,16,128]{3,2,1,0:T(8,128)} %refs_1_.1, f32[16,16,128]{2,1,0:T(8,128)} %refs_2_.1, f32[3,8,8,128]{3,2,1,0:T(8,128)} %refs_3_.1, s32[16,16]{1,0:T(8,128)} %refs_4_.1, f32[16,16,128]{2,1,0:T(8,128)} %refs_5_.1), custom_call_target="tpu_custom_call" | custom-call | tf_op jit(solution)/shard_map/pallas_call | solution.py:386
  25.9 4.1 %shard_map.86 = (f32[3,16,16,128]{3,2,1,0:T(8,128)}, f32[6,16,16,128]{3,2,1,0:T(8,128)}, f32[16,16,128]{2,1,0:T(8,128)}) custom-call(f32[3,18,32,128]{3,2,1,0:T(8,128)} %get-tuple-element.5.field, f32[17,32,128]{2,1,0:T(8,128)} %get-tuple-element.6.cons), custom_call_target="tpu_custom_call" | custom-call | tf_op jit(solution)/shard_map/pallas_call | solution.py:413

commit v7 on v6

--- a/solution.py
+++ b/solution.py
@@ -46,7 +46,8 @@
 def smooth(sizes, *refs):
     nx, ny, depth, kx, ky, slabs, planes = sizes
     (start_hbm, load_hbm, shift_hbm, coarse_hbm, agg_hbm, cons_hbm, final, cons,
-     start, load, shift, table, agg, earlier, resid, resid_sent, in_sem, send_sem, recv_sem) = refs
+     start, load, shift, table, agg, earlier, resid, resid_sent, smoothed,
+     in_sem, send_sem, recv_sem) = refs
     fields = [earlier.at[n] for n in range(DEGREE)]
     slab = lax.axis_index("slab")
     plane = lax.axis_index("plane")
@@ -156,7 +157,18 @@
     first_go = (field_edge(fields[0], 2), 4)
     middle_go = (field_edge(fields[2], 2), 5)
     resid_go = (field_edge(resid_sent, 1), 6)
-    final_go = (field_edge(final, 1), 7)
+
+    def final_edge(step_x, step_y):
+        from_x, to_x = edge(step_x, 1, nx)
+        from_y, to_y = edge(step_y, OFF, ny)
+        from_x = pl.ds(from_x.start - 1, from_x.size)
+        from_y = pl.ds(from_y.start - OFF, from_y.size)
+        return smoothed.at[:, from_x, from_y], final.at[:, to_x, to_y]
+
+    final_go = (final_edge, 7)
+    own_final = pltpu.make_async_copy(
+        smoothed, final.at[:, pl.ds(1, nx), pl.ds(OFF, ny)], in_sem.at[6]
+    )
     start_all(*coarse_go)
     start_all(*load_go)
     start_all(*shift_go)
@@ -259,7 +271,7 @@
             else:
                 for n in range(DEGREE):
                     direction = direction + fields[n][inner]
-                final[where] = direction
+                smoothed[c] = direction
             return carry
 
         if phase % 2 == 0:
@@ -270,16 +282,19 @@
             start_all(*middle_go)
             start_all(*resid_go)
     start_all(*final_go)
+    own_final.start()
 
     loads[3].wait()
     wait_arrived(*cons_go)
     for go in (coarse_go, load_go, shift_go, cons_go, first_go, middle_go, resid_go):
         wait_sent(*go)
+    own_final.wait()
     wait_arrived(*final_go)
     wait_sent(*final_go)
 
 
-def stresses(sizes, field, cons, disp_out, rec_out, ind_out, rec, ind, out_sem):
+def stresses(sizes, field_hbm, cons_hbm, disp_out, rec_out, ind_out,
+             field, cons, rec, ind, in_sem, out_sem):
     nx, ny, depth, kx, ky, slabs, planes = sizes
     first_x = lax.axis_index("slab") * nx
     first_y = lax.axis_index("plane") * ny
@@ -296,7 +311,23 @@
 
     scale_y = half((node_y >= 1) & (node_y <= total_y - 2)) * half((lane >= 1) & (lane <= depth - 2))
 
-    inner = field.at[:, pl.ds(1, nx), pl.ds(OFF, ny)]
+    def arriving(n):
+        lines = pl.ds(OFF - 1, ny + 2)
+        nodes = pl.ds(n * ROWS_OUT + 2, ROWS_OUT) if n else pl.ds(0, ROWS_OUT + 2)
+        corners = pl.ds(n * ROWS_OUT + 1, ROWS_OUT) if n else pl.ds(0, ROWS_OUT + 1)
+        return (
+            pltpu.make_async_copy(
+                field_hbm.at[:, nodes, lines], field.at[:, nodes, lines], in_sem.at[2 * n]
+            ),
+            pltpu.make_async_copy(
+                cons_hbm.at[corners, lines], cons.at[corners, lines], in_sem.at[2 * n + 1]
+            ),
+        )
+
+    for n in range(nx // ROWS_OUT):
+        for copy in arriving(n):
+            copy.start()
+    inner = field_hbm.at[:, pl.ds(1, nx), pl.ds(OFF, ny)]
     whole = pltpu.make_async_copy(inner, disp_out, out_sem.at[0])
     whole.start()
 
@@ -363,8 +394,12 @@
         )
         return after
 
-    carry = element_row(0)
+    carry = None
     for n in range(nx // ROWS_OUT):
+        for copy in arriving(n):
+            copy.wait()
+        if n == 0:
+            carry = element_row(0)
         carry = lax.fori_loop(1 + n * ROWS_OUT, 1 + (n + 1) * ROWS_OUT, row, carry, unroll=True)
         for copy in part(n):
             copy.start()
@@ -377,7 +412,6 @@
 def body(sizes, *blocks):
     nx, ny, depth, kx, ky, slabs, planes = sizes
     hbm = pl.BlockSpec(memory_space=pltpu.HBM)
-    vmem = pl.BlockSpec(memory_space=pltpu.VMEM)
     f32 = jnp.float32
     padded = (
         jax.ShapeDtypeStruct((3, nx + 2, ny + 16, depth), f32),
@@ -387,7 +421,7 @@
         functools.partial(smooth, sizes),
         out_shape=padded,
         in_specs=[hbm] * 6,
-        out_specs=(vmem,) * 2,
+        out_specs=(hbm,) * 2,
         scratch_shapes=[
             pltpu.VMEM((3, nx, ny, depth), f32),
             pltpu.VMEM((3, nx + 2, ny + 16, depth), f32),
@@ -397,7 +431,8 @@
             pltpu.VMEM((DEGREE, 3, nx + 4, ny + 16, depth), f32),
             pltpu.VMEM((3, nx + 2, ny + 16, depth), f32),
             pltpu.VMEM((3, nx + 2, ny + 16, depth), f32),
-            pltpu.SemaphoreType.DMA((6,)),
+            pltpu.VMEM((3, nx, ny, depth), f32),
+            pltpu.SemaphoreType.DMA((7,)),
             pltpu.SemaphoreType.DMA((8, len(SIDES))),
             pltpu.SemaphoreType.DMA((8, len(SIDES))),
         ],
@@ -413,11 +448,14 @@
     return pl.pallas_call(
         functools.partial(stresses, sizes),
         out_shape=outs,
-        in_specs=[vmem] * 2,
+        in_specs=[hbm] * 2,
         out_specs=(hbm,) * 3,
         scratch_shapes=[
+            pltpu.VMEM(padded[0].shape, f32),
+            pltpu.VMEM(padded[1].shape, f32),
             pltpu.VMEM(outs[1].shape, f32),
             pltpu.VMEM(outs[2].shape, f32),
+            pltpu.SemaphoreType.DMA((2 * (nx // ROWS_OUT),)),
             pltpu.SemaphoreType.DMA((1 + 2 * (nx // ROWS_OUT),)),
         ],
         compiler_params=pltpu.CompilerParams(vmem_limit_bytes=VMEM_BYTES),

time: 30.1 us -> 38.3 us (1.27)
  Pallas kernels: 29.3 us -> 37.5 us
    pallas_call x1, Pallas kernels: 4.12 us -> 13.2 us  [body(): pl.pallas_call(functools.partial(stresses, sizes), out_shape=outs, in_spe...]
    pallas_call x1, Pallas kernels: 25.2 us -> 24.3 us  [body(): pl.pallas_call(functools.partial(smooth, sizes), out_shape=padded, in_spe...]
where the time goes in v7:
time: 38.3 us; the launch traced here: 38.2 us
  Pallas kernels  37.5 us (98%)
  between operations  0.64 us (2%)
    pallas_call x1, Pallas kernels, body(): pl.pallas_call(functools.partial(smooth, sizes), out_shape=padded, in_spe...  24.3 us
    pallas_call x1, Pallas kernels, body(): pl.pallas_call(functools.partial(stresses, sizes), out_shape=outs, in_spe...  13.2 us

profile of v7, /device:TPU:0, one launch (start us, length us, event | category | flops | bytes accessed | tf_op | source)
XLA Modules:
  0.0 38.2 jit_solution(15101137518722486440)
XLA Ops:
  0.6 24.3 %shard_map.85 = (f32[3,18,32,128]{3,2,1,0:T(8,128)}, f32[17,32,128]{2,1,0:T(8,128)}) custom-call(f32[3,16,16,128]{3,2,1,0:T(8,128)} %refs_0_.1, f32[3,16,16,128]{3,2,1,0:T(8,128)} %refs_1_.1, f32[16,16,128]{2,1,0:T(8,128)} %refs_2_.1, f32[3,8,8,128]{3,2,1,0:T(8,128)} %refs_3_.1, s32[16,16]{1,0:T(8,128)} %refs_4_.1, f32[16,16,128]{2,1,0:T(8,128)} %refs_5_.1), custom_call_target="tpu_custom_call" | custom-call | tf_op jit(solution)/shard_map/pallas_call | solution.py:420
  25.0 13.2 %shard_map.86 = (f32[3,16,16,128]{3,2,1,0:T(8,128)}, f32[6,16,16,128]{3,2,1,0:T(8,128)}, f32[16,16,128]{2,1,0:T(8,128)}) custom-call(f32[3,18,32,128]{3,2,1,0:T(8,128)} %get-tuple-element.5.field_hbm, f32[17,32,128]{2,1,0:T(8,128)} %get-tuple-element.6.cons_hbm), custom_call_target="tpu_custom_call" | custom-call | tf_op jit(solution)/shard_map/pallas_call | solution.py:448

commit v8 on v7

--- a/solution.py
+++ b/solution.py
@@ -327,15 +327,18 @@
     for n in range(nx // ROWS_OUT):
         for copy in arriving(n):
             copy.start()
-    inner = field_hbm.at[:, pl.ds(1, nx), pl.ds(OFF, ny)]
-    whole = pltpu.make_async_copy(inner, disp_out, out_sem.at[0])
-    whole.start()
+
+    def displaced(n):
+        return pltpu.make_async_copy(
+            field.at[:, pl.ds(n * ROWS_OUT + 1, ROWS_OUT), pl.ds(OFF, ny)],
+            disp_out.at[:, pl.ds(n * ROWS_OUT, ROWS_OUT)], out_sem.at[3 * n],
+        )
 
     def part(n):
         here = pl.ds(n * ROWS_OUT, ROWS_OUT)
         return (
-            pltpu.make_async_copy(rec.at[:, here], rec_out.at[:, here], out_sem.at[1 + 2 * n]),
-            pltpu.make_async_copy(ind.at[here], ind_out.at[here], out_sem.at[2 + 2 * n]),
+            pltpu.make_async_copy(rec.at[:, here], rec_out.at[:, here], out_sem.at[3 * n + 1]),
+            pltpu.make_async_copy(ind.at[here], ind_out.at[here], out_sem.at[3 * n + 2]),
         )
 
     def corner_sums(c, i):
@@ -398,13 +401,14 @@
     for n in range(nx // ROWS_OUT):
         for copy in arriving(n):
             copy.wait()
+        displaced(n).start()
         if n == 0:
             carry = element_row(0)
         carry = lax.fori_loop(1 + n * ROWS_OUT, 1 + (n + 1) * ROWS_OUT, row, carry, unroll=True)
         for copy in part(n):
             copy.start()
-    whole.wait()
     for n in range(nx // ROWS_OUT):
+        displaced(n).wait()
         for copy in part(n):
             copy.wait()
 
@@ -456,7 +460,7 @@
             pltpu.VMEM(outs[1].shape, f32),
             pltpu.VMEM(outs[2].shape, f32),
             pltpu.SemaphoreType.DMA((2 * (nx // ROWS_OUT),)),
-            pltpu.SemaphoreType.DMA((1 + 2 * (nx // ROWS_OUT),)),
+            pltpu.SemaphoreType.DMA((3 * (nx // ROWS_OUT),)),
         ],
         compiler_params=pltpu.CompilerParams(vmem_limit_bytes=VMEM_BYTES),
     )(field, cons)

time: 38.3 us -> 28.6 us (0.75)
  Pallas kernels: 37.5 us -> 27.8 us
    pallas_call x1, Pallas kernels: 13.2 us -> 3.44 us  [body(): pl.pallas_call(functools.partial(stresses, sizes), out_shape=outs, in_spe...]
where the time goes in v8:
time: 28.6 us; the launch traced here: 28.4 us
  Pallas kernels  27.8 us (97%)
  between operations  0.64 us (2%)
    pallas_call x1, Pallas kernels, body(): pl.pallas_call(functools.partial(smooth, sizes), out_shape=padded, in_spe...  24.3 us
    pallas_call x1, Pallas kernels, body(): pl.pallas_call(functools.partial(stresses, sizes), out_shape=outs, in_spe...  3.44 us

profile of v8, /device:TPU:0, one launch (start us, length us, event | category | flops | bytes accessed | tf_op | source)
XLA Modules:
  0.0 28.4 jit_solution(7414686029123380130)
XLA Ops:
  0.6 24.3 %shard_map.85 = (f32[3,18,32,128]{3,2,1,0:T(8,128)}, f32[17,32,128]{2,1,0:T(8,128)}) custom-call(f32[3,16,16,128]{3,2,1,0:T(8,128)} %refs_0_.1, f32[3,16,16,128]{3,2,1,0:T(8,128)} %refs_1_.1, f32[16,16,128]{2,1,0:T(8,128)} %refs_2_.1, f32[3,8,8,128]{3,2,1,0:T(8,128)} %refs_3_.1, s32[16,16]{1,0:T(8,128)} %refs_4_.1, f32[16,16,128]{2,1,0:T(8,128)} %refs_5_.1), custom_call_target="tpu_custom_call" | custom-call | tf_op jit(solution)/shard_map/pallas_call | solution.py:424
  25.0 3.4 %shard_map.86 = (f32[3,16,16,128]{3,2,1,0:T(8,128)}, f32[6,16,16,128]{3,2,1,0:T(8,128)}, f32[16,16,128]{2,1,0:T(8,128)}) custom-call(f32[3,18,32,128]{3,2,1,0:T(8,128)} %get-tuple-element.5.field_hbm, f32[17,32,128]{2,1,0:T(8,128)} %get-tuple-element.6.cons_hbm), custom_call_target="tpu_custom_call" | custom-call | tf_op jit(solution)/shard_map/pallas_call | solution.py:452

commit v9 on v8

--- a/solution.py
+++ b/solution.py
@@ -66,8 +66,8 @@
         ),
         pltpu.make_async_copy(shift_hbm, shift.at[pl.ds(1, nx), pl.ds(OFF, ny)], in_sem.at[5]),
     ]
-    for copy in loads:
-        copy.start()
+    for n in (0, 1, 2, 4, 5, 3):
+        loads[n].start()
 
     zero_table = jnp.zeros((3, 8, depth), jnp.float32)
     for a in range(kx + 2):
@@ -275,9 +275,9 @@
             return carry
 
         if phase % 2 == 0:
-            lax.fori_loop(0, 6, wide, 0)
+            lax.fori_loop(0, 6, wide, 0, unroll=True)
         else:
-            lax.fori_loop(0, 3, narrow, 0)
+            lax.fori_loop(0, 3, narrow, 0, unroll=True)
         if phase == 1:
             start_all(*middle_go)
             start_all(*resid_go)

time: 28.6 us -> 27.1 us (0.948)
  Pallas kernels: 27.8 us -> 26.4 us
    pallas_call x1, Pallas kernels: 24.3 us -> 22.9 us  [body(): pl.pallas_call(functools.partial(smooth, sizes), out_shape=padded, in_spe...]
where the time goes in v9:
time: 27.1 us; the launch traced here: 27 us
  Pallas kernels  26.4 us (97%)
  between operations  0.64 us (2%)
    pallas_call x1, Pallas kernels, body(): pl.pallas_call(functools.partial(smooth, sizes), out_shape=padded, in_spe...  22.9 us
    pallas_call x1, Pallas kernels, body(): pl.pallas_call(functools.partial(stresses, sizes), out_shape=outs, in_spe...  3.44 us

profile of v9, /device:TPU:0, one launch (start us, length us, event | category | flops | bytes accessed | tf_op | source)
XLA Modules:
  0.0 27.0 jit_solution(7419386064045957028)
XLA Ops:
  0.6 22.9 %shard_map.85 = (f32[3,18,32,128]{3,2,1,0:T(8,128)}, f32[17,32,128]{2,1,0:T(8,128)}) custom-call(f32[3,16,16,128]{3,2,1,0:T(8,128)} %refs_0_.1, f32[3,16,16,128]{3,2,1,0:T(8,128)} %refs_1_.1, f32[16,16,128]{2,1,0:T(8,128)} %refs_2_.1, f32[3,8,8,128]{3,2,1,0:T(8,128)} %refs_3_.1, s32[16,16]{1,0:T(8,128)} %refs_4_.1, f32[16,16,128]{2,1,0:T(8,128)} %refs_5_.1), custom_call_target="tpu_custom_call" | custom-call | tf_op jit(solution)/shard_map/pallas_call | solution.py:424
  23.6 3.4 %shard_map.86 = (f32[3,16,16,128]{3,2,1,0:T(8,128)}, f32[6,16,16,128]{3,2,1,0:T(8,128)}, f32[16,16,128]{2,1,0:T(8,128)}) custom-call(f32[3,18,32,128]{3,2,1,0:T(8,128)} %get-tuple-element.5.field_hbm, f32[17,32,128]{2,1,0:T(8,128)} %get-tuple-element.6.cons_hbm), custom_call_target="tpu_custom_call" | custom-call | tf_op jit(solution)/shard_map/pallas_call | solution.py:452

commit v10 on v9

--- a/solution.py
+++ b/solution.py
@@ -172,7 +172,6 @@
     start_all(*coarse_go)
     start_all(*load_go)
     start_all(*shift_go)
-    start_all(*cons_go)
 
     loads[1].wait()
     cols = ky * planes
@@ -206,6 +205,7 @@
         fields[0][c, 2:nx + 2, OFF:OFF + ny, :] = start[c] + moved.reshape(nx, ny, depth)
 
     start_all(*first_go)
+    start_all(*cons_go)
     loads[4].wait()
     loads[5].wait()
     wait_arrived(*load_go)

time: 27.1 us -> 27.3 us (level)
  no operation moved by 1% of the time
where the time goes in v10:
time: 27.3 us; the launch traced here: 27.2 us
  Pallas kernels  26.6 us (97%)
  between operations  0.64 us (2%)
    pallas_call x1, Pallas kernels, body(): pl.pallas_call(functools.partial(smooth, sizes), out_shape=padded, in_spe...  23.1 us
    pallas_call x1, Pallas kernels, body(): pl.pallas_call(functools.partial(stresses, sizes), out_shape=outs, in_spe...  3.44 us

profile of v10, /device:TPU:0, one launch (start us, length us, event | category | flops | bytes accessed | tf_op | source)
XLA Modules:
  0.0 27.2 jit_solution(3625682125899974480)
XLA Ops:
  0.6 23.1 %shard_map.85 = (f32[3,18,32,128]{3,2,1,0:T(8,128)}, f32[17,32,128]{2,1,0:T(8,128)}) custom-call(f32[3,16,16,128]{3,2,1,0:T(8,128)} %refs_0_.1, f32[3,16,16,128]{3,2,1,0:T(8,128)} %refs_1_.1, f32[16,16,128]{2,1,0:T(8,128)} %refs_2_.1, f32[3,8,8,128]{3,2,1,0:T(8,128)} %refs_3_.1, s32[16,16]{1,0:T(8,128)} %refs_4_.1, f32[16,16,128]{2,1,0:T(8,128)} %refs_5_.1), custom_call_target="tpu_custom_call" | custom-call | tf_op jit(solution)/shard_map/pallas_call | solution.py:424
  23.7 3.4 %shard_map.86 = (f32[3,16,16,128]{3,2,1,0:T(8,128)}, f32[6,16,16,128]{3,2,1,0:T(8,128)}, f32[16,16,128]{2,1,0:T(8,128)}) custom-call(f32[3,18,32,128]{3,2,1,0:T(8,128)} %get-tuple-element.5.field_hbm, f32[17,32,128]{2,1,0:T(8,128)} %get-tuple-element.6.cons_hbm), custom_call_target="tpu_custom_call" | custom-call | tf_op jit(solution)/shard_map/pallas_call | solution.py:452
